TPU v7x, 32 devices: a whole 2x2x4 slice. The times are simulated.
32 devices in a mesh: ctx: 4 (over z), row: 4 (over y, x), col: 2 (over core).
Axes of the slice: x: 2, y: 2, z: 4, core: 2. Of those that a mesh axis runs over, the one named last changes fastest.
Arguments:
- patches: bfloat16 [3072, 2048], P(('ctx', 'row'), 'col'), may hold values from -6 to 6
- visible: int32 [3072], P(('ctx', 'row')), may hold values from -1 to 262143, as said below
- ln_gain: float32 [2048], replicated, may hold values from 0.1 to 1.9
- ln_bias: float32 [2048], replicated, may hold values from -3 to 3
- w_query: bfloat16 [2048, 2048], P('row', 'col')
- w_key: bfloat16 [2048, 2048], P('row', 'col')
- w_value: bfloat16 [2048, 2048], P('row', 'col'), may hold values from -0.125 to 0.125
- w_output: bfloat16 [2048, 2048], P('row', 'col'), may hold values from -0.375 to 0.375
Outputs:
- attn_out: float32 [3072, 2048], P(('ctx', 'row'), 'col')
Inputs may be any that keep to these rules, and one draw needn't show every extreme that they name: Slots s * 768 to (s + 1) * 768 - 1 form slab s: first the distinct visible patch numbers of that slab in increasing order, all in s * 65536 to (s + 1) * 65536 - 1, then -1 in every remaining slot. Each slab holds 384 or more visible patches, and some slab is full.
All inputs are finite; a program needn't handle non-finite values.
Results may differ from a plain program's by a relative error of at most 0.0094.
Values may be sent and summed in bfloat16 or wider, within the bound.
A program may use at most 128 MiB of HBM per device.

v0:
```python
import math

import jax
import jax.numpy as jnp
from jax import lax
from jax.sharding import PartitionSpec as P

HEAD_DIM = 128
GRID = 64


def embed(visible, full_width):
    patch_id = jnp.maximum(visible, 0)
    plane_size = GRID * GRID
    coord_x = (patch_id // plane_size).astype(jnp.float32)
    coord_y = (patch_id // GRID % GRID).astype(jnp.float32)
    coord_z = (patch_id % GRID).astype(jnp.float32)
    channel = jnp.arange(full_width, dtype=jnp.int32)
    axis_pick = channel % 3
    frequency = jnp.exp(-math.log(10000.0) * (channel // 6 * 6).astype(jnp.float32) / full_width)
    offset_phase = 0.5 * math.pi * (channel // 3 % 2).astype(jnp.float32)
    picked = jnp.where(
        axis_pick[None, :] == 0,
        coord_x[:, None],
        jnp.where(axis_pick[None, :] == 1, coord_y[:, None], coord_z[:, None]),
    )
    return jnp.sin(picked * frequency[None, :] + offset_phase[None, :])


def normalize(hidden, ln_gain, ln_bias):
    center = hidden - jnp.mean(hidden, axis=1, keepdims=True)
    spread = jnp.mean(center * center, axis=1, keepdims=True)
    return (center * lax.rsqrt(spread + 1e-06) * ln_gain[None, :] + ln_bias[None, :]).astype(
        jnp.bfloat16
    )


def body(patches, visible, ln_gain, ln_bias, w_query, w_key, w_value, w_output):
    rows_full = lax.all_gather(patches, "col", axis=1, tiled=True)
    local_rows = rows_full.shape[0]
    hidden = rows_full.astype(jnp.float32) + embed(visible, rows_full.shape[1])
    normed = normalize(hidden, ln_gain, ln_bias)
    col_width = w_query.shape[1]
    slab_rows = lax.all_gather(normed, "row", axis=0, tiled=True)
    input_start = lax.axis_index("row") * w_query.shape[0]
    own_inputs = lax.dynamic_slice_in_dim(slab_rows, input_start, w_query.shape[0], 1)
    joined = jnp.concatenate([w_query, w_key, w_value], axis=1)
    summed = lax.psum_scatter(
        jnp.dot(own_inputs, joined, preferred_element_type=jnp.float32),
        "row",
        scatter_dimension=0,
        tiled=True,
    )
    query_f = summed[:, :col_width]
    key_f = summed[:, col_width : 2 * col_width]
    value_f = summed[:, 2 * col_width :]
    head_count = col_width // HEAD_DIM
    query = (
        (query_f * (1.0 / math.sqrt(HEAD_DIM)))
        .astype(jnp.bfloat16)
        .reshape(local_rows, head_count, HEAD_DIM)
    )
    keys = key_f.astype(jnp.bfloat16)
    values = value_f.astype(jnp.bfloat16)
    key_live = (visible >= 0).astype(jnp.bfloat16)
    best = jnp.full((head_count, local_rows), -1e30, jnp.float32)
    key_piece = lax.all_gather(keys, ("ctx", "row"), axis=0, tiled=True)
    value_piece = lax.all_gather(values, ("ctx", "row"), axis=0, tiled=True)
    live_piece = lax.all_gather(key_live, ("ctx", "row"), axis=0, tiled=True)
    count = key_piece.shape[0]
    scores = jnp.einsum(
        "qhd,nhd->hqn",
        query,
        key_piece.reshape(count, head_count, HEAD_DIM),
        preferred_element_type=jnp.float32,
    )
    scores = jnp.where(live_piece[None, None, :] > 0, scores, -1e30)
    new_best = jnp.maximum(best, jnp.max(scores, axis=2))
    weights = jnp.exp(scores - new_best[:, :, None])
    totals = jnp.sum(weights, axis=2)
    accum = jnp.einsum(
        "hqn,nhd->hqd",
        weights.astype(jnp.bfloat16),
        value_piece.reshape(count, head_count, HEAD_DIM),
        preferred_element_type=jnp.float32,
    )
    best, totals, accum = (new_best, totals, accum)
    mixed = (
        (accum / totals[:, :, None])
        .transpose(1, 0, 2)
        .reshape(local_rows, col_width)
        .astype(jnp.bfloat16)
    )
    mixed_full = lax.all_gather(mixed, "col", axis=1, tiled=True)
    return jnp.dot(
        mixed_full,
        lax.all_gather(w_output, "row", axis=0, tiled=True),
        preferred_element_type=jnp.float32,
    )


def solution(mesh):
    placed = (
        P(("ctx", "row"), "col"),
        P(("ctx", "row")),
        P(),
        P(),
        P("row", "col"),
        P("row", "col"),
        P("row", "col"),
        P("row", "col"),
    )
    return jax.shard_map(
        body, mesh=mesh, in_specs=placed, out_specs=P(("ctx", "row"), "col"), check_vma=False
    )
```

profile of v0, /device:TPU:1, one launch (start us, length us, event | category | flops | bytes accessed | tf_op | source)
XLA Modules:
  0.0 433.3 jit_solution(2298070488895586865)
XLA Ops:
  6.6 0.8 fusion.60
  7.4 2.7 all_gather.22
  10.1 5.7 %fusion.23 = f32[192]{0:T(256)S(1)} fusion(bf16[192,2048]{1,0:T(8,128)(2,1)S(1)} %all_gather.22, f32[2048]{0:T(1024)S(1)} %get-tuple-element.13, f32[2048]{0:T(1024)S(1)} %get-tuple-element.12, f32[192]{0:T(256)S(1)} %get-tuple-element.9, f32[192]{0:T(256)S(1)} %get-tuple-element.8, f32[192]{0:T(256)S(1)} %get-tuple-element.7, ...), kind=kLoop, calls=%fused_computation.23 | loop fusion | flops 2752320 | bytes 809984 | tf_op jit(solution)/shard_map/reduce_sum | solution.py:31
  15.8 5.8 %multiply_reduce_fusion = f32[192]{0:T(256)S(1)} fusion(bf16[192,2048]{1,0:T(8,128)(2,1)S(1)} %all_gather.22, f32[192]{0:T(256)S(1)} %broadcast_multiply_fusion, f32[2048]{0:T(1024)S(1)} %get-tuple-element.13, f32[2048]{0:T(1024)S(1)} %get-tuple-element.12, f32[192]{0:T(256)S(1)} %get-tuple-element.9, f32[192]{0:T(256)S(1)} %get-tuple-element.8, ...), kind=kLoop, calls=%fused_computation.20 | loop fusion | flops 3538752 | bytes 810752 | tf_op jit(solution)/shard_map/reduce_sum | solution.py:32
  21.6 0.2 add_rsqrt_fusion
  21.8 7.4 %add_convert_fusion = bf16[192,2048]{1,0:T(8,128)(2,1)} fusion(bf16[192,2048]{1,0:T(8,128)(2,1)S(1)} %all_gather.22, f32[2048]{0:T(1024)} %param.11, f32[2048]{0:T(1024)} %param.10, f32[192]{0:T(256)S(1)} %add_rsqrt_fusion, f32[192]{0:T(256)S(1)} %broadcast_multiply_fusion, f32[2048]{0:T(1024)S(1)} %get-tuple-element.13, f32[2048]{0:T(1024)S(1)} %get-tuple-element.12, ...), kind=kLoop, calls=%fused_computation.19 | loop fusion | flops 4325376 | bytes 1613568 | tf_op jit(solution)/shard_map/convert_element_type | solution.py:33
  29.2 0.0 all-gather.5.cloned.1.call-update
  29.3 0.0 reduce-scatter.2.cloned.1.call-start
  29.3 46.2 %all-gather.5.cloned.1.call-done = bf16[768,2048]{1,0:T(8,128)(2,1)} async-done(((bf16[192,2048]{1,0:T(8,128)(2,1)}), bf16[768,2048]{1,0:T(8,128)(2,1)}) %all-gather.5.cloned.1.call-update) | async-done | bytes 3145744 | tf_op jit(solution)/shard_map/all_gather | solution.py:44
  75.5 6.5 %fusion.12 = f32[768,3072]{1,0:T(8,128)} fusion(bf16[512,1024]{1,0:T(8,128)(2,1)S(1)} %copy-done.1, bf16[512,1024]{1,0:T(8,128)(2,1)S(1)} %copy-done.2, bf16[512,1024]{1,0:T(8,128)(2,1)S(1)} %copy-done.3, bf16[768,2048]{1,0:T(8,128)(2,1)} %all-gather.5.cloned.1.call-done, s32[]{:T(128)S(6)} %select_n.83), kind=kOutput, calls=%fused_computation.13 | convolution fusion | flops 2425356288 | bytes 13369348 | tf_op jit(solution)/shard_map/dot_general | solution.py:49
  82.0 0.0 reduce-scatter.2.cloned.1.call-update
  82.0 0.0 all-gather.7.cloned.1.call-start
  82.1 95.1 %reduce-scatter.2.cloned.1.call-done = f32[192,3072]{1,0:T(8,128)} async-done(((f32[768,3072]{1,0:T(8,128)}), f32[192,3072]{1,0:T(8,128)}) %reduce-scatter.2.cloned.1.call-update) | async-done | bytes 2359312 | tf_op jit(solution)/shard_map/reduce_scatter | solution.py:48
  177.1 1.8 convert.4
  179.0 0.9 fusion.67
  179.9 0.0 all-gather.7.cloned.1.call-update
  179.9 0.0 all-gather.9.cloned.1.call-start
  180.0 0.5 all-gather.9.cloned.1.call-update
  180.5 0.0 all-gather.11.cloned.1.call-start
  180.5 0.5 all-gather.11.cloned.1.call-update
  181.1 0.6 dynamic-slice
  182.3 0.2 dynamic-update-slice
  182.5 34.7 %all-reduce = bf16[3072]{0:T(1024)(128)(2,1)S(1)} all-reduce(bf16[3072]{0:T(1024)(128)(2,1)S(1)} %dynamic-update-slice), channel_id=1, replica_groups=mesh['ctx'=4,'row'=4,'col'=2] {'ctx','row'}, use_global_device_ids=true, to_apply=%add | all-reduce | flops 3072 | bytes 12288
  217.3 56.5 %all-gather.7.cloned.1.call-done = bf16[3072,1024]{1,0:T(8,128)(2,1)} async-done(((bf16[192,1024]{1,0:T(8,128)(2,1)}), bf16[3072,1024]{1,0:T(8,128)(2,1)}) %all-gather.7.cloned.1.call-update) | async-done | bytes 6291472 | tf_op jit(solution)/shard_map/all_gather | solution.py:67
  273.8 12.3 %select_reduce_fusion = (f32[8,192]{1,0:T(8,128)S(1)}, f32[8,192,3072]{2,1,0:T(8,128)}) fusion(pred[3072]{0:T(1024)(128)(4,1)S(1)} %broadcast_compare_fusion, bf16[3072,1024]{1,0:T(8,128)(2,1)} %all-gather.7.cloned.1.call-done, f32[192,3072]{1,0:T(8,128)} %reduce-scatter.2.cloned.1.call-done), kind=kOutput, calls=%fused_computation.1 | convolution fusion | flops 1217788416 | bytes 25961472 | tf_op jit(solution)/shard_map/qhd,nhd->hqn/dot_general | solution.py:71
  286.1 9.8 %fusion = f32[8,192]{1,0:T(8,128)S(1)} fusion(f32[8,192,3072]{2,1,0:T(8,128)} %get-tuple-element.11, f32[8,192]{1,0:T(8,128)S(1)} %broadcast_maximum_fusion, pred[3072]{0:T(1024)(128)(4,1)S(1)} %broadcast_compare_fusion), kind=kLoop, calls=%fused_computation.2 | loop fusion | flops 14154240 | bytes 18889728 | tf_op jit(solution)/shard_map/reduce_sum | solution.py:80
  295.9 72.9 %all-gather.9.cloned.1.call-done = bf16[3072,1024]{1,0:T(8,128)(2,1)} async-done(((bf16[192,1024]{1,0:T(8,128)(2,1)}), bf16[3072,1024]{1,0:T(8,128)(2,1)}) %all-gather.9.cloned.1.call-update) | async-done | bytes 6291472 | tf_op jit(solution)/shard_map/all_gather | solution.py:68
  368.8 10.8 %fusion.34 = bf16[8,24,8,128]{3,2,1,0:T(8,128)(2,1)S(1)} fusion(f32[8,192,3072]{2,1,0:T(8,128)} %get-tuple-element.11, f32[8,192]{1,0:T(8,128)S(1)} %broadcast_maximum_fusion, pred[3072]{0:T(1024)(128)(4,1)S(1)} %broadcast_compare_fusion, f32[192,8]{0,1:T(8,128)S(1)} %bitcast.51, bf16[3072,1024]{1,0:T(8,128)(2,1)} %all-gather.9.cloned.1.call-done), kind=kOutput, calls=%fused_computation.26 | convolution fusion | flops 1222508544 | bytes 25574400 | tf_op jit(solution)/shard_map/hqn,nhd->hqd/dot_general | solution.py:81
  379.7 0.1 copy.45
  379.8 4.5 %all_gather.26 = bf16[192,2048]{1,0:T(8,128)(2,1)S(1)} all-gather(bf16[192,1024]{1,0:T(8,128)(2,1)S(1)} %bitcast.50), channel_id=1, replica_groups=mesh['ctx'=4,'row'=4,'col'=2] {'col'}, dimensions={1}, use_global_device_ids=true | all-gather | bytes 1179648 | tf_op jit(solution)/shard_map/all_gather | solution.py:94
  384.3 38.5 %all-gather.11.cloned.1.call-done = bf16[2048,1024]{1,0:T(8,128)(2,1)} async-done(((bf16[512,1024]{1,0:T(8,128)(2,1)}), bf16[2048,1024]{1,0:T(8,128)(2,1)}) %all-gather.11.cloned.1.call-update) | async-done | bytes 4194320 | tf_op jit(solution)/shard_map/all_gather | solution.py:97
  422.7 4.1 fusion.68
  (18 shorter events, 0.1 us)
Async XLA Ops:
  6.5 68.9 %copy-start.3 = (bf16[512,1024]{1,0:T(8,128)(2,1)S(1)}, bf16[512,1024]{1,0:T(8,128)(2,1)}, u32[]{:S(2)}) copy-start(bf16[512,1024]{1,0:T(8,128)(2,1)} %param.12) | copy-start | bytes 3145732
  6.5 68.9 %copy-start.2 = (bf16[512,1024]{1,0:T(8,128)(2,1)S(1)}, bf16[512,1024]{1,0:T(8,128)(2,1)}, u32[]{:S(2)}) copy-start(bf16[512,1024]{1,0:T(8,128)(2,1)} %param.13) | copy-start | bytes 3145732
  6.5 68.9 %copy-start.1 = (bf16[512,1024]{1,0:T(8,128)(2,1)S(1)}, bf16[512,1024]{1,0:T(8,128)(2,1)}, u32[]{:S(2)}) copy-start(bf16[512,1024]{1,0:T(8,128)(2,1)} %param.14) | copy-start | bytes 3145732
  6.5 68.9 %all-gather.5.cloned.1.call-start = ((), (), s32[]{:S(2)}) async-start(), calls=%async_computation.1 | async-start | bytes 3932160 | tf_op jit(solution)/shard_map/all_gather | solution.py:44
  29.3 147.9 %reduce-scatter.2.cloned.1.call-start = ((), (), s32[]{:S(2)}) async-start(), calls=%async_computation.2 | async-start | bytes 11796480 | tf_op jit(solution)/shard_map/reduce_scatter | solution.py:48
  82.0 99.1 %copy-start.4 = (u32[32]{0:T(128)S(1)}, u32[32]{0:T(128)}, u32[]{:S(2)}) copy-start(u32[32]{0:T(128)} %constant.122) | copy-start | bytes 388
  82.0 100.2 %copy-start = (s32[192]{0:T(256)S(1)}, s32[192]{0:T(256)}, u32[]{:S(2)}) copy-start(s32[192]{0:T(256)} %param.9) | copy-start | bytes 2308
  82.0 191.7 %all-gather.7.cloned.1.call-start = ((), (), s32[]{:S(2)}) async-start(), calls=%async_computation.3 | async-start | bytes 6684672 | tf_op jit(solution)/shard_map/all_gather | solution.py:67
  179.9 188.9 %all-gather.9.cloned.1.call-start = ((), (), s32[]{:S(2)}) async-start(), calls=%async_computation.4 | async-start | bytes 6684672 | tf_op jit(solution)/shard_map/all_gather | solution.py:68
  180.5 242.2 %all-gather.11.cloned.1.call-start = ((), (), s32[]{:S(2)}) async-start(), calls=%async_computation.5 | async-start | bytes 5242880 | tf_op jit(solution)/shard_map/all_gather | solution.py:97
Sparse Core Ops, SparseCore 0:
  29.4 46.0 all-gather.4
  82.1 94.9 reduce-scatter.1
  180.0 93.6 all-gather.6
  276.4 92.3 all-gather.8
  370.5 52.1 all-gather.10
where the time goes:
time: 434 us; the launch traced here: 433 us
  waiting for transfers between devices  310 us (71%)
  blocking collectives  41.9 us (10%)
  matrix products  33.7 us (8%)
  other arithmetic  31.6 us (7%)
  between operations  13.8 us (3%)
    reduce_scatter x1, waiting for transfers between devices, body(): lax.psum_scatter(jnp.dot(own_inputs, joined, preferred_element_type=jnp.f...  95.1 us
    all_gather x1, waiting for transfers between devices, body(): value_piece = lax.all_gather(values, ('ctx', 'row'), axis=0, tiled=True)  72.9 us
    all_gather x1, waiting for transfers between devices, body(): key_piece = lax.all_gather(keys, ('ctx', 'row'), axis=0, tiled=True)  56.5 us
    all_gather x1, waiting for transfers between devices, body(): slab_rows = lax.all_gather(normed, 'row', axis=0, tiled=True)  46.2 us
    all_gather x1, waiting for transfers between devices, body(): lax.all_gather(w_output, 'row', axis=0, tiled=True)  38.5 us
    unnamed x1, blocking collectives  34.7 us
    dot_general x1, matrix products, body(): jnp.einsum('qhd,nhd->hqn', query, key_piece.reshape(count, head_count, HE...  12.3 us
    dot_general x1, matrix products, body(): jnp.einsum('hqn,nhd->hqd', weights.astype(jnp.bfloat16), value_piece.resh...  10.8 us
  transfers between devices with their start and end apart: 5, of which 5 were waited for; matrix products, arithmetic and copies ran while one was open for 8% of the time, Pallas kernels for 0%

commit v1 on v0

--- a/solution.py
+++ b/solution.py
@@ -1,12 +1,17 @@
+import functools
 import math
 
 import jax
 import jax.numpy as jnp
 from jax import lax
+from jax.experimental import pallas as pl
+from jax.experimental.pallas import tpu as pltpu
 from jax.sharding import PartitionSpec as P
 
 HEAD_DIM = 128
 GRID = 64
+MESH = pl.DeviceIdType.MESH
+DEAD = -1e30
 
 
 def embed(visible, full_width):
@@ -99,6 +104,388 @@
     )
 
 
+def mesh_kernel(
+    sizes, patches, vis, chan, gain, bias, live, w_query, w_key, w_value, w_output, out,
+    pfull, hid, wfull, wo, xs, lives, send, queries, kv, key_bias, scores, probs, mixed, mrec, parts, got,
+    p_sem, wo_sem, w_send, w_recv, w_near, w_own, wf_sem, x_sem, l_send, l_recv,
+    a_send, a_recv, f_send, f_recv, m_send, m_recv, o_send, o_recv,
+):
+    Z, R, hd = sizes
+    z, r, c = lax.axis_index("ctx"), lax.axis_index("row"), lax.axis_index("col")
+    half, full_width = xs.shape[0] // Z, xs.shape[1]
+    depth, cw = w_query.shape
+    plane = wfull.shape[2]
+    other = 1 - c
+
+    def device(zz, rr, cc):
+        return {"ctx": zz, "row": rr, "col": cc}
+
+    def push(src, dst, ssem, rsem, dev):
+        copy = pltpu.make_async_remote_copy(
+            src_ref=src, dst_ref=dst, send_sem=ssem, recv_sem=rsem, device_id=dev, device_id_type=MESH
+        )
+        copy.start()
+        return copy
+
+    def landed(ref, sem):
+        pltpu.make_async_copy(ref, ref, sem).wait()
+
+    sibling = device(z, r, other)
+    barrier = pltpu.get_barrier_semaphore()
+    for oz in range(Z):
+        for orow in range(R):
+            for oc in range(2):
+                if (oz, orow, oc) != (0, 0, 0) and (oc == 0 or oz == 0):
+                    pl.semaphore_signal(
+                        barrier,
+                        inc=1,
+                        device_id=device(lax.rem(z + oz, Z), lax.rem(r + orow, R), lax.rem(c + oc, 2)),
+                        device_id_type=MESH,
+                    )
+    pl.semaphore_wait(barrier, Z * R - 1 + R)
+
+    sent = [
+        push(
+            patches.at[pl.ds(pl.multiple_of(other * half, half), half)],
+            pfull.at[c], p_sem.at[0], p_sem.at[1], sibling,
+        )
+    ]
+    weights = (w_key, w_value, w_query)
+    owner = (z * plane) // cw
+    col0 = pl.multiple_of(lax.rem(z * plane, cw), plane)
+    sub = depth // 2
+
+    def weight_copies(i):
+        src = weights[i]
+        copies = []
+        for o in range(1, R):
+            for cc in range(2):
+                copies.append(
+                    pltpu.make_async_remote_copy(
+                        src_ref=src.at[pl.ds(cc * sub, sub), pl.ds(col0, plane)],
+                        dst_ref=wfull.at[i, pl.ds(pl.multiple_of(r * depth + cc * sub, sub), sub)],
+                        send_sem=w_send.at[i, o, cc],
+                        recv_sem=w_recv.at[i, o],
+                        device_id=device(z, lax.rem(r + o, R), cc),
+                        device_id_type=MESH,
+                    )
+                )
+        own = wfull.at[i, pl.ds(pl.multiple_of(r * depth, depth), depth)]
+        copies.append(
+            pltpu.make_async_remote_copy(
+                src_ref=src.at[:, pl.ds(col0, plane)], dst_ref=own,
+                send_sem=w_send.at[i, 0, 0], recv_sem=w_near.at[i],
+                device_id=sibling, device_id_type=MESH,
+            )
+        )
+        return copies, pltpu.make_async_copy(src.at[:, pl.ds(col0, plane)], own, w_own.at[i])
+
+    @pl.when(c == owner)
+    def _():
+        for i in range(3):
+            copies, local = weight_copies(i)
+            for copy in copies:
+                copy.start()
+            local.start()
+
+    wo_copy = pltpu.make_async_copy(w_output, wo.at[c], wo_sem.at[2])
+    wo_copy.start()
+    sent.append(push(w_output, wo.at[c], wo_sem.at[0], wo_sem.at[1], sibling))
+    me = z * R + r
+    for oz in range(Z):
+        for orow in range(R):
+            if (oz, orow) != (0, 0):
+                sent.append(
+                    push(
+                        live, lives.at[me], l_send.at[oz * R + orow], l_recv.at[oz * R + orow],
+                        device(lax.rem(z + oz, Z), lax.rem(r + orow, R), c),
+                    )
+                )
+    lives[me] = live[...]
+
+    row0 = pl.multiple_of(c * half, half)
+    pfull[c] = patches[pl.ds(row0, half), :]
+
+    def embed_rows(t, carry):
+        at = pl.multiple_of(t * 8, 8)
+        patch_id = jnp.maximum(vis[pl.ds(row0 + at, 8), :], 0)
+        coord_x = (patch_id >> 12).astype(jnp.float32)
+        coord_y = ((patch_id >> 6) & (GRID - 1)).astype(jnp.float32)
+        coord_z = (patch_id & (GRID - 1)).astype(jnp.float32)
+        pick = chan[2:3, :]
+        coord = jnp.where(pick == 0.0, coord_x, jnp.where(pick == 1.0, coord_y, coord_z))
+        hid[pl.ds(at, 8), :] = jnp.sin(coord * chan[0:1, :] + chan[1:2, :])
+        return carry
+
+    lax.fori_loop(0, half // 8, embed_rows, 0)
+    landed(pfull.at[other], p_sem.at[1])
+    own_slab = pl.multiple_of(z * half, half)
+
+    def norm_rows(t, carry):
+        at = pl.multiple_of(t * 16, 16)
+        rows = pl.ds(at, 16)
+        embedded = jnp.concatenate([pfull[0, rows, :], pfull[1, rows, :]], axis=1)
+        hidden = embedded.astype(jnp.float32) + hid[rows, :]
+        center = hidden - jnp.mean(hidden, axis=1, keepdims=True)
+        spread = jnp.mean(center * center, axis=1, keepdims=True)
+        normed = center * lax.rsqrt(spread + 1e-06) * gain[...] + bias[...]
+        xs[pl.ds(own_slab + at, 16), :] = normed.astype(jnp.bfloat16)
+        return carry
+
+    lax.fori_loop(0, half // 16, norm_rows, 0)
+    for oz in range(1, Z):
+        slab = xs.at[pl.ds(own_slab, half)]
+        sent.append(push(slab, slab, x_sem.at[0, oz], x_sem.at[1, oz], device(lax.rem(z + oz, Z), r, c)))
+
+    for oz in range(Z):
+        for orow in range(R):
+            if (oz, orow) != (0, 0):
+                src = lax.rem(z + Z - oz, Z) * R + lax.rem(r + R - orow, R)
+                landed(lives.at[src], l_recv.at[oz * R + orow])
+    columns = lives[...].reshape(Z * R * 8, 128).T
+    for zz in range(Z):
+        for rr in range(R):
+            for cc in range(2):
+                at = (zz * R + rr) * 8 + cc
+                key_bias[cc, rr, zz * half : (zz + 1) * half, :] = columns[:half, at : at + 1]
+
+    for i in range(3):
+        for o in range(1, R):
+            src_row = lax.rem(r + R - o, R)
+            block = wfull.at[i, pl.ds(pl.multiple_of(src_row * depth + c * sub, sub), sub)]
+            landed(block, w_recv.at[i, o])
+            sent.append(push(block, block, wf_sem.at[0, i, o], wf_sem.at[1, i, o], sibling))
+    for oz in range(1, Z):
+        slab = xs.at[pl.ds(pl.multiple_of(lax.rem(z + Z - oz, Z) * half, half), half)]
+        landed(slab, x_sem.at[1, oz])
+
+    scale = 1.0 / math.sqrt(hd)
+    for i in range(3):
+        mine = wfull.at[i, pl.ds(pl.multiple_of(r * depth, depth), depth)]
+
+        @pl.when(c == owner)
+        def _():
+            landed(mine, w_own.at[i])
+
+        @pl.when(c != owner)
+        def _():
+            landed(mine, w_near.at[i])
+
+        for o in range(1, R):
+            src_row = lax.rem(r + R - o, R)
+            block = wfull.at[i, pl.ds(pl.multiple_of(src_row * depth + other * sub, sub), sub)]
+            landed(block, wf_sem.at[1, i, o])
+        for j in range(0, R, 2):
+            pair = jnp.dot(
+                xs[...], wfull[i, :, j * hd : (j + 2) * hd], preferred_element_type=jnp.float32
+            )
+            if i == 2:
+                pair = pair * scale
+            pair = pair.astype(jnp.bfloat16)
+            send[i, j] = pair[:, :hd]
+            send[i, j + 1] = pair[:, hd:]
+        for o in range(1, R):
+            j = lax.rem(r + o, R)
+            dst = queries.at[r] if i == 2 else kv.at[i, c, r]
+            sent.append(push(send.at[i, j], dst, a_send.at[i, o], a_recv.at[i, o], device(z, j, c)))
+        if i == 2:
+            queries[r] = send[i, r]
+        else:
+            kv[i, c, r] = send[i, r]
+            sent.append(push(send.at[i, r], kv.at[i, c, r], f_send.at[i, 0], f_recv.at[i, 0], sibling))
+    for i in range(2):
+        for o in range(1, R):
+            block = kv.at[i, c, lax.rem(r + R - o, R)]
+            landed(block, a_recv.at[i, o])
+            sent.append(push(block, block, f_send.at[i, o], f_recv.at[i, o], sibling))
+    for o in range(1, R):
+        landed(queries.at[lax.rem(r + R - o, R)], a_recv.at[2, o])
+    for i in range(2):
+        for o in range(R):
+            landed(kv.at[i, other, lax.rem(r + R - o, R)], f_recv.at[i, o])
+
+    count = xs.shape[0]
+    head = z * R + r
+    group = head // Z
+    lane0 = pl.multiple_of(lax.rem(head, Z) * hd, hd)
+
+    def mixed_copy(block, zz):
+        return pltpu.make_async_remote_copy(
+            src_ref=mixed.at[block, pl.ds(zz * half, half)],
+            dst_ref=mrec.at[block, :, pl.ds(lane0, hd)],
+            send_sem=m_send.at[block, zz],
+            recv_sem=m_recv.at[lax.rem(head, Z), block],
+            device_id=device(zz, group, c),
+            device_id_type=MESH,
+        )
+
+    def attend(block, carry):
+        query = queries[block]
+        best = jnp.full((1, count), DEAD, jnp.float32)
+        for cc in range(2):
+            for rr in range(R):
+                score = lax.dot_general(
+                    kv[0, cc, rr], query, (((1,), (1,)), ((), ())), preferred_element_type=jnp.float32
+                )
+                score = score + key_bias[cc, rr]
+                scores[cc, rr] = score
+                best = jnp.maximum(best, jnp.max(score, axis=0, keepdims=True))
+        totals = jnp.zeros((1, count), jnp.float32)
+        accum = jnp.zeros((hd, count), jnp.float32)
+        for cc in range(2):
+            for rr in range(R):
+                weight = jnp.exp(scores[cc, rr] - best)
+                totals = totals + jnp.sum(weight, axis=0, keepdims=True)
+                accum = accum + lax.dot_general(
+                    kv[1, cc, rr], weight.astype(jnp.bfloat16), (((0,), (0,)), ((), ())),
+                    preferred_element_type=jnp.float32,
+                )
+        mixed[block] = (accum / totals).T.astype(jnp.bfloat16)
+        for zz in range(Z):
+            here = jnp.logical_and(z == zz, group == r)
+
+            @pl.when(jnp.logical_not(here))
+            def _():
+                mixed_copy(block, zz).start()
+
+            @pl.when(here)
+            def _():
+                mrec[block, :, pl.ds(lane0, hd)] = mixed[block, pl.ds(zz * half, half), :]
+
+        return carry
+
+    lax.fori_loop(0, R, attend, 0)
+    for block in range(R):
+        for k in range(Z):
+            @pl.when(r * Z + k != head)
+            def _():
+                landed(mrec.at[block, :, pl.ds(k * hd, hd)], m_recv.at[k, block])
+
+    wo_copy.wait()
+    landed(wo.at[other], wo_sem.at[1])
+    for cc in range(2):
+        part = jnp.dot(
+            mrec[...].reshape(R * half, depth), wo[cc], preferred_element_type=jnp.float32
+        )
+        parts[cc] = part.astype(jnp.bfloat16).reshape(R, half, cw)
+    for o in range(1, R):
+        for oc in range(2):
+            j, cc = lax.rem(r + o, R), lax.rem(c + oc, 2)
+            sent.append(
+                push(parts.at[cc, j], got.at[r, c], o_send.at[o, oc], o_recv.at[o, oc], device(z, j, cc))
+            )
+    sent.append(push(parts.at[other, r], got.at[r, c], o_send.at[0, 1], o_recv.at[0, 1], sibling))
+    got[r, c] = parts[c, r]
+    for o in range(R):
+        for oc in range(2):
+            if (o, oc) != (0, 0):
+                landed(got.at[lax.rem(r + R - o, R), lax.rem(c + oc, 2)], o_recv.at[o, oc])
+    for cc in range(2):
+        total = got[0, cc].astype(jnp.float32)
+        for rr in range(1, R):
+            total = total + got[rr, cc].astype(jnp.float32)
+        out[cc * half : (cc + 1) * half, :] = total
+
+    for copy in sent:
+        copy.wait_send()
+
+    @pl.when(c == owner)
+    def _():
+        for i in range(3):
+            for copy in weight_copies(i)[0]:
+                copy.wait_send()
+
+    for block in range(R):
+        for zz in range(Z):
+            @pl.when(jnp.logical_not(jnp.logical_and(z == zz, group == r)))
+            def _():
+                mixed_copy(block, zz).wait_send()
+
+
+def fused(sizes, patches, visible, ln_gain, ln_bias, w_query, w_key, w_value, w_output):
+    Z, R = sizes
+    rows, cw = patches.shape
+    depth = w_query.shape[0]
+    width = depth * R
+    half = rows // 2
+    hd = HEAD_DIM
+    plane = R * hd
+    count = Z * half
+    channel = jnp.arange(width, dtype=jnp.int32)
+    chan = jnp.stack(
+        [
+            jnp.exp(-math.log(10000.0) * (channel // 6 * 6).astype(jnp.float32) / width),
+            0.5 * math.pi * (channel // 3 % 2).astype(jnp.float32),
+            (channel % 3).astype(jnp.float32),
+        ]
+    )
+    live = jnp.where(visible >= 0, 0.0, DEAD).astype(jnp.float32).reshape(2, half)
+    live = jnp.pad(live, ((0, 6), (0, 128 - half)))
+    vmem = pl.BlockSpec(memory_space=pltpu.VMEM)
+    hbm = pl.BlockSpec(memory_space=pl.ANY)
+    bf, f32, dma = jnp.bfloat16, jnp.float32, pltpu.SemaphoreType.DMA
+    return pl.pallas_call(
+        functools.partial(mesh_kernel, (Z, R, hd)),
+        out_shape=jax.ShapeDtypeStruct((rows, cw), f32),
+        in_specs=[vmem] * 6 + [hbm] * 4,
+        out_specs=vmem,
+        scratch_shapes=[
+            pltpu.VMEM((2, half, cw), bf),
+            pltpu.VMEM((half, width), f32),
+            pltpu.VMEM((3, width, plane), bf),
+            pltpu.VMEM((2, depth, cw), bf),
+            pltpu.VMEM((count, width), bf),
+            pltpu.VMEM((Z * R, 8, 128), f32),
+            pltpu.VMEM((3, R, count, hd), bf),
+            pltpu.VMEM((R, count, hd), bf),
+            pltpu.VMEM((2, 2, R, count, hd), bf),
+            pltpu.VMEM((2, R, count, 1), f32),
+            pltpu.VMEM((2, R, count, count), f32),
+            pltpu.VMEM((2, R, count, count), bf),
+            pltpu.VMEM((R, count, hd), bf),
+            pltpu.VMEM((R, half, depth), bf),
+            pltpu.VMEM((2, R, half, cw), bf),
+            pltpu.VMEM((R, 2, half, cw), bf),
+            dma((2,)),
+            dma((3,)),
+            dma((3, R, 2)),
+            dma((3, R)),
+            dma((3,)),
+            dma((3,)),
+            dma((2, 3, R)),
+            dma((2, Z)),
+            dma((Z * R,)),
+            dma((Z * R,)),
+            dma((3, R)),
+            dma((3, R)),
+            dma((2, R)),
+            dma((2, R)),
+            dma((R, Z)),
+            dma((Z, R)),
+            dma((R, 2)),
+            dma((R, 2)),
+        ],
+        compiler_params=pltpu.CompilerParams(
+            collective_id=0, has_side_effects=True, vmem_limit_bytes=56 * 1024 * 1024
+        ),
+    )(patches, visible.reshape(rows, 1), chan, ln_gain.reshape(1, width), ln_bias.reshape(1, width),
+      live, w_query, w_key, w_value, w_output)
+
+
+def fits(mesh, patches, w_query):
+    Z, R, C = mesh.shape["ctx"], mesh.shape["row"], mesh.shape["col"]
+    width = w_query.shape[0]
+    half = patches.shape[0] // (Z * R * 2)
+    return (
+        C == 2
+        and Z * R * HEAD_DIM == width
+        and (width // C) % (R * HEAD_DIM) == 0
+        and width // R == Z * HEAD_DIM
+        and half % 16 == 0
+        and half <= 128
+    )
+
+
 def solution(mesh):
     placed = (
         P(("ctx", "row"), "col"),
@@ -110,6 +497,13 @@
         P("row", "col"),
         P("row", "col"),
     )
-    return jax.shard_map(
-        body, mesh=mesh, in_specs=placed, out_specs=P(("ctx", "row"), "col"), check_vma=False
-    )
+
+    def run(*args):
+        part = body
+        if fits(mesh, args[0], args[4]):
+            part = functools.partial(fused, (mesh.shape["ctx"], mesh.shape["row"]))
+        return jax.shard_map(
+            part, mesh=mesh, in_specs=placed, out_specs=P(("ctx", "row"), "col"), check_vma=False
+        )(*args)
+
+    return run

time: 434 us -> 102 us (0.24)
  waiting for transfers between devices: 310 us -> 0 us
  Pallas kernels: 0 us -> 96.9 us
  blocking collectives: 41.9 us -> 0 us
  matrix products: 33.7 us -> 0 us
  other arithmetic: 31.6 us -> 0.72 us
  between operations: 13.8 us -> 0.02 us
    all_gather x4 -> x0, waiting for transfers between devices: 214 us -> none  [the longest x1 72.9 us: body(): value_piece = lax.all_gather(values, ('ctx', 'row'), axis=0, tiled=True)]
    pallas_call x0 -> x1, Pallas kernels: none -> 96.9 us  [fused(): pl.pallas_call(functools.partial(mesh_kernel, (Z, R, hd)), out_shape=jax....]
    reduce_scatter x1 -> x0, waiting for transfers between devices: 95.1 us -> none  [body(): lax.psum_scatter(jnp.dot(own_inputs, joined, preferred_element_type=jnp.f...]
    unnamed x1 -> x0, blocking collectives: 34.7 us -> none
    dot_general x4 -> x0, matrix products: 33.7 us -> none  [the longest x1 12.3 us: body(): jnp.einsum('qhd,nhd->hqn', query, key_piece.reshape(count, head_count, HE...]
    reduce_sum x3 -> x0, other arithmetic: 21.3 us -> none  [the longest x1 9.83 us: body(): totals = jnp.sum(weights, axis=2)]
    convert_element_type x3 -> x1, other arithmetic: 8.25 us -> 0.03 us  [fused(): (channel % 3).astype(jnp.float32)]
    all_gather x2 -> x0, blocking collectives: 7.23 us -> none  [the longest x1 4.52 us: body(): mixed_full = lax.all_gather(mixed, 'col', axis=1, tiled=True)]
  transfers between devices with their start and end apart: 5 -> 0, of which waited for: 5 -> 0; matrix products, arithmetic and copies ran while one was open for 8% -> 0% of each run, Pallas kernels for 0% -> 0%
where the time goes in v1:
time: 102 us
  Pallas kernels  96.9 us (95%)
  local copies, waits for them, and re-layouts  4.21 us (4%)
    pallas_call x1, Pallas kernels, fused(): pl.pallas_call(functools.partial(mesh_kernel, (Z, R, hd)), out_shape=jax....  96.9 us
    unnamed x3, local copies, waits for them, and re-layouts  2.77 us

profile of v1, /device:TPU:1, one launch (start us, length us, event | category | flops | bytes accessed | tf_op | source)
XLA Modules:
  0.0 101.8 jit_solution(5220015215085066255)
XLA Ops:
  0.0 0.0 copy-start
  0.0 0.7 copy-done
  0.7 0.1 reshape.141
  0.8 0.6 pad.4.live
  1.4 0.1 fusion.4
  1.5 0.6 pad_maximum_fusion.chan
  2.1 0.8 copy.9.vis
  2.9 96.9 %shard_map.82 = f32[192,1024]{1,0:T(8,128)} custom-call(bf16[192,1024]{1,0:T(8,128)(2,1)} %patches.1, s32[192,1]{1,0:T(8,128)} %copy.9.vis, f32[3,2048]{1,0:T(4,128)} %pad_maximum_fusion.chan, f32[1,2048]{1,0:T(1,128)} %bitcast.3, f32[1,2048]{1,0:T(1,128)} %bitcast.4, f32[8,128]{1,0:T(8,128)} %pad.4.live, bf16[512,1024]{1,0:T(8,128)(2,1)} %w_query.1, ...), custom_call_target="tpu_custom_call" | custom-call | tf_op jit(solution)/shard_map/pallas_call | solution.py:427
  99.8 2.1 %copy.11 = f32[192,1024]{1,0:T(8,128)} copy(f32[192,1024]{1,0:T(8,128)} %shard_map.82) | data formatting | bytes 1572864
  (2 shorter events, 0.0 us)
Async XLA Ops:
  0.0 0.7 copy-start

commit v2 on v1

v2 whole, which is shorter than its diff:
```python
import functools
import math

import jax
import jax.numpy as jnp
from jax import lax
from jax.experimental import pallas as pl
from jax.experimental.pallas import tpu as pltpu
from jax.sharding import PartitionSpec as P

HEAD_DIM = 128
GRID = 64
MESH = pl.DeviceIdType.MESH
DEAD = -1e30
STEP = 32


def embed(visible, full_width):
    patch_id = jnp.maximum(visible, 0)
    plane_size = GRID * GRID
    coord_x = (patch_id // plane_size).astype(jnp.float32)
    coord_y = (patch_id // GRID % GRID).astype(jnp.float32)
    coord_z = (patch_id % GRID).astype(jnp.float32)
    channel = jnp.arange(full_width, dtype=jnp.int32)
    axis_pick = channel % 3
    frequency = jnp.exp(-math.log(10000.0) * (channel // 6 * 6).astype(jnp.float32) / full_width)
    offset_phase = 0.5 * math.pi * (channel // 3 % 2).astype(jnp.float32)
    picked = jnp.where(
        axis_pick[None, :] == 0,
        coord_x[:, None],
        jnp.where(axis_pick[None, :] == 1, coord_y[:, None], coord_z[:, None]),
    )
    return jnp.sin(picked * frequency[None, :] + offset_phase[None, :])


def normalize(hidden, ln_gain, ln_bias):
    center = hidden - jnp.mean(hidden, axis=1, keepdims=True)
    spread = jnp.mean(center * center, axis=1, keepdims=True)
    return (center * lax.rsqrt(spread + 1e-06) * ln_gain[None, :] + ln_bias[None, :]).astype(
        jnp.bfloat16
    )


def body(patches, visible, ln_gain, ln_bias, w_query, w_key, w_value, w_output):
    rows_full = lax.all_gather(patches, "col", axis=1, tiled=True)
    local_rows = rows_full.shape[0]
    hidden = rows_full.astype(jnp.float32) + embed(visible, rows_full.shape[1])
    normed = normalize(hidden, ln_gain, ln_bias)
    col_width = w_query.shape[1]
    slab_rows = lax.all_gather(normed, "row", axis=0, tiled=True)
    input_start = lax.axis_index("row") * w_query.shape[0]
    own_inputs = lax.dynamic_slice_in_dim(slab_rows, input_start, w_query.shape[0], 1)
    joined = jnp.concatenate([w_query, w_key, w_value], axis=1)
    summed = lax.psum_scatter(
        jnp.dot(own_inputs, joined, preferred_element_type=jnp.float32),
        "row",
        scatter_dimension=0,
        tiled=True,
    )
    query_f = summed[:, :col_width]
    key_f = summed[:, col_width : 2 * col_width]
    value_f = summed[:, 2 * col_width :]
    head_count = col_width // HEAD_DIM
    query = (
        (query_f * (1.0 / math.sqrt(HEAD_DIM)))
        .astype(jnp.bfloat16)
        .reshape(local_rows, head_count, HEAD_DIM)
    )
    keys = key_f.astype(jnp.bfloat16)
    values = value_f.astype(jnp.bfloat16)
    key_live = (visible >= 0).astype(jnp.bfloat16)
    best = jnp.full((head_count, local_rows), -1e30, jnp.float32)
    key_piece = lax.all_gather(keys, ("ctx", "row"), axis=0, tiled=True)
    value_piece = lax.all_gather(values, ("ctx", "row"), axis=0, tiled=True)
    live_piece = lax.all_gather(key_live, ("ctx", "row"), axis=0, tiled=True)
    count = key_piece.shape[0]
    scores = jnp.einsum(
        "qhd,nhd->hqn",
        query,
        key_piece.reshape(count, head_count, HEAD_DIM),
        preferred_element_type=jnp.float32,
    )
    scores = jnp.where(live_piece[None, None, :] > 0, scores, -1e30)
    new_best = jnp.maximum(best, jnp.max(scores, axis=2))
    weights = jnp.exp(scores - new_best[:, :, None])
    totals = jnp.sum(weights, axis=2)
    accum = jnp.einsum(
        "hqn,nhd->hqd",
        weights.astype(jnp.bfloat16),
        value_piece.reshape(count, head_count, HEAD_DIM),
        preferred_element_type=jnp.float32,
    )
    best, totals, accum = (new_best, totals, accum)
    mixed = (
        (accum / totals[:, :, None])
        .transpose(1, 0, 2)
        .reshape(local_rows, col_width)
        .astype(jnp.bfloat16)
    )
    mixed_full = lax.all_gather(mixed, "col", axis=1, tiled=True)
    return jnp.dot(
        mixed_full,
        lax.all_gather(w_output, "row", axis=0, tiled=True),
        preferred_element_type=jnp.float32,
    )


def mesh_kernel(
    sizes, patches, vis, gain, bias, w_query, w_key, w_value, w_output, got,
    ids, id_col, pin, pnear, hid, wfull, wo, xs, send, queries, kv, key_bias, scores, mixed, mrec, parts,
    p_own, z_send, z_recv, near_send, near_recv, wo_sem, w_send, w_recv, w_near, w_own, wf_sem,
    l_send, l_recv, a_send, a_recv, f_send, f_recv, m_send, m_recv, o_send, o_recv, o_own,
):
    Z, R, hd = sizes
    z, r, c = lax.axis_index("ctx"), lax.axis_index("row"), lax.axis_index("col")
    count, full_width = xs.shape
    half = count // Z
    depth, cw = w_query.shape
    plane = wfull.shape[2]
    other = 1 - c
    blocks = half // STEP
    f32, bf16 = jnp.float32, jnp.bfloat16

    def device(zz, rr, cc):
        return {"ctx": zz, "row": rr, "col": cc}

    def remote(src, dst, ssem, rsem, dev):
        return pltpu.make_async_remote_copy(
            src_ref=src, dst_ref=dst, send_sem=ssem, recv_sem=rsem, device_id=dev, device_id_type=MESH
        )

    sent = []

    def push(src, dst, ssem, rsem, dev):
        copy = remote(src, dst, ssem, rsem, dev)
        copy.start()
        sent.append(copy)

    def landed(ref, sem):
        pltpu.make_async_copy(ref, ref, sem).wait()

    sibling = device(z, r, other)
    barrier = pltpu.get_barrier_semaphore()
    for oz in range(Z):
        for orow in range(R):
            for oc in range(2):
                if (oz, orow, oc) != (0, 0, 0) and (oc == 0 or oz == 0):
                    pl.semaphore_signal(
                        barrier,
                        inc=1,
                        device_id=device(lax.rem(z + oz, Z), lax.rem(r + orow, R), lax.rem(c + oc, 2)),
                        device_id_type=MESH,
                    )
    own_patches = pltpu.make_async_copy(patches, pin.at[z], p_own)
    own_patches.start()
    wo_copy = pltpu.make_async_copy(w_output, wo.at[c], wo_sem.at[2])
    wo_copy.start()
    me = z * R + r
    ids[me] = jnp.zeros((8, 128), jnp.int32)
    ids[me, 0:1, 0:half] = vis[:, 0:half]
    ids[me, 1:2, 0:half] = vis[:, half : 2 * half]
    channel = lax.broadcasted_iota(jnp.int32, (1, full_width), 1)
    sixth = channel // 6
    third = channel // 3
    frequency = jnp.exp(-math.log(10000.0) * (sixth * 6).astype(f32) / full_width)
    phase = 0.5 * math.pi * (third % 2).astype(f32)
    pick = channel - third * 3
    pl.semaphore_wait(barrier, Z * R - 1 + R)

    for oz in range(Z):
        for orow in range(R):
            if (oz, orow) != (0, 0):
                push(
                    ids.at[me], ids.at[me], l_send.at[oz * R + orow], l_recv.at[oz * R + orow],
                    device(lax.rem(z + oz, Z), lax.rem(r + orow, R), c),
                )

    def hop(up, far):
        slab = z - far if up else z + far
        block = pin.at[slab]
        src = patches if far == 0 else block
        way = 0 if up else 1
        return remote(
            src, block, z_send.at[way, far], z_recv.at[way, far + 1], device(z + 1 if up else z - 1, r, c)
        )

    def passes(up, far):
        return jnp.logical_and(z >= far, z < Z - 1) if up else jnp.logical_and(z + far < Z, z > 0)

    for up in (True, False):
        @pl.when(passes(up, 0))
        def _():
            hop(up, 0).start()

    weights = (w_key, w_value, w_query)
    owner = (z * plane) // cw
    col0 = pl.multiple_of(lax.rem(z * plane, cw), plane)
    sub = depth // 2

    def weight_copies(i):
        src = weights[i]
        copies = []
        for o in range(1, R):
            for cc in range(2):
                copies.append(
                    remote(
                        src.at[pl.ds(cc * sub, sub), pl.ds(col0, plane)],
                        wfull.at[i, pl.ds(pl.multiple_of(r * depth + cc * sub, sub), sub)],
                        w_send.at[i, o, cc],
                        w_recv.at[i, o],
                        device(z, lax.rem(r + o, R), cc),
                    )
                )
        own = wfull.at[i, pl.ds(pl.multiple_of(r * depth, depth), depth)]
        copies.append(
            remote(src.at[:, pl.ds(col0, plane)], own, w_send.at[i, 0, 0], w_near.at[i], sibling)
        )
        return copies

    def weight_local(i):
        own = wfull.at[i, pl.ds(pl.multiple_of(r * depth, depth), depth)]
        return pltpu.make_async_copy(weights[i].at[:, pl.ds(col0, plane)], own, w_own.at[i])

    @pl.when(c == owner)
    def _():
        for i in range(3):
            for copy in weight_copies(i):
                copy.start()
            weight_local(i).start()

    push(w_output, wo.at[c], wo_sem.at[0], wo_sem.at[1], sibling)
    own_patches.wait()

    def share(slab):
        push(
            pin.at[slab, pl.ds(pl.multiple_of(other * half, half), half)],
            pnear.at[slab], near_send.at[slab], near_recv.at[slab], sibling,
        )

    share(z)

    for oz in range(Z):
        for orow in range(R):
            if (oz, orow) != (0, 0):
                src = lax.rem(z + Z - oz, Z) * R + lax.rem(r + R - orow, R)
                landed(ids.at[src], l_recv.at[oz * R + orow])
    for zz in range(Z):
        columns = ids[zz * R + r].astype(f32).T
        id_col[zz * half : (zz + 1) * half, :] = jnp.where(
            c == 0, columns[:half, 0:1], columns[:half, 1:2]
        )

    def embed_rows(base):
        def run(t, carry):
            at = pl.multiple_of(base + t * 8, 8)
            patch_id = jnp.maximum(id_col[pl.ds(at, 8), :].astype(jnp.int32), 0)
            coord_x = (patch_id >> 12).astype(f32)
            coord_y = ((patch_id >> 6) & (GRID - 1)).astype(f32)
            coord_z = (patch_id & (GRID - 1)).astype(f32)
            coord = jnp.where(pick == 0, coord_x, jnp.where(pick == 1, coord_y, coord_z))
            hid[pl.ds(at, 8), :] = jnp.sin(coord * frequency + phase)
            return carry

        lax.fori_loop(0, half // 8, run, 0)

    row0 = pl.multiple_of(c * half, half)

    def norm_slab(slab):
        landed(pnear.at[slab], near_recv.at[slab])
        base = pl.multiple_of(slab * half, half)

        def run(t, carry):
            at = pl.multiple_of(t * 16, 16)
            mine = pin[slab, pl.ds(row0 + at, 16), :]
            theirs = pnear[slab, pl.ds(at, 16), :]
            left = jnp.where(c == 0, mine, theirs)
            right = jnp.where(c == 0, theirs, mine)
            embedded = jnp.concatenate([left, right], axis=1)
            hidden = embedded.astype(f32) + hid[pl.ds(base + at, 16), :]
            center = hidden - jnp.mean(hidden, axis=1, keepdims=True)
            spread = jnp.mean(center * center, axis=1, keepdims=True)
            normed = center * lax.rsqrt(spread + 1e-06) * gain[...] + bias[...]
            xs[pl.ds(base + at, 16), :] = normed.astype(bf16)
            return carry

        lax.fori_loop(0, half // 16, run, 0)

    embed_rows(0)
    embed_rows(half)
    for far in range(1, Z):
        for up in (True, False):
            slab = z - far if up else z + far

            @pl.when(z >= far if up else z + far < Z)
            def _():
                landed(pin.at[slab], z_recv.at[0 if up else 1, far])

            if far < Z - 1:
                @pl.when(passes(up, far))
                def _():
                    hop(up, far).start()

            @pl.when(z >= far if up else z + far < Z)
            def _():
                remote(
                    pin.at[slab, pl.ds(pl.multiple_of(other * half, half), half)],
                    pnear.at[slab], near_send.at[slab], near_recv.at[slab], sibling,
                ).start()

        if far == 1:
            for zz in range(2, Z):
                embed_rows(zz * half)
            columns = ids[...].astype(f32).reshape(Z * R * 8, 128).T
            dead = jnp.where(columns < 0.0, DEAD, 0.0)
            for zz in range(Z):
                for rr in range(R):
                    for cc in range(2):
                        at = (zz * R + rr) * 8 + cc
                        key_bias[cc, rr, zz * half : (zz + 1) * half, :] = dead[:half, at : at + 1]
            norm_slab(z)
        for up in (True, False):
            slab = z - far if up else z + far

            @pl.when(z >= far if up else z + far < Z)
            def _():
                norm_slab(slab)

    for i in range(3):
        for o in range(1, R):
            src_row = lax.rem(r + R - o, R)
            block = wfull.at[i, pl.ds(pl.multiple_of(src_row * depth + c * sub, sub), sub)]
            landed(block, w_recv.at[i, o])
            push(block, block, wf_sem.at[0, i, o], wf_sem.at[1, i, o], sibling)

    scale = 1.0 / math.sqrt(hd)
    for i in range(3):
        mine = wfull.at[i, pl.ds(pl.multiple_of(r * depth, depth), depth)]

        @pl.when(c == owner)
        def _():
            landed(mine, w_own.at[i])

        @pl.when(c != owner)
        def _():
            landed(mine, w_near.at[i])

        for o in range(1, R):
            src_row = lax.rem(r + R - o, R)
            block = wfull.at[i, pl.ds(pl.multiple_of(src_row * depth + other * sub, sub), sub)]
            landed(block, wf_sem.at[1, i, o])
        for j in range(0, R, 2):
            pair = jnp.dot(
                xs[...], wfull[i, :, j * hd : (j + 2) * hd], preferred_element_type=f32
            )
            if i == 2:
                pair = pair * scale
            pair = pair.astype(bf16)
            if i == 2:
                pair = jnp.concatenate(
                    [
                        pair[zz * half + b * STEP : zz * half + (b + 1) * STEP]
                        for b in range(blocks)
                        for zz in range(Z)
                    ],
                    axis=0,
                )
            send[i, j] = pair[:, :hd]
            send[i, j + 1] = pair[:, hd:]
        for o in range(1, R):
            j = lax.rem(r + o, R)
            dst = queries.at[r] if i == 2 else kv.at[i, c, r]
            push(send.at[i, j], dst, a_send.at[i, o], a_recv.at[i, o], device(z, j, c))
        if i == 2:
            queries[r] = send[i, r]
        else:
            kv[i, c, r] = send[i, r]
            push(send.at[i, r], kv.at[i, c, r], f_send.at[i, 0], f_recv.at[i, 0], sibling)
    for i in range(2):
        for o in range(1, R):
            block = kv.at[i, c, lax.rem(r + R - o, R)]
            landed(block, a_recv.at[i, o])
            push(block, block, f_send.at[i, o], f_recv.at[i, o], sibling)
    for o in range(1, R):
        landed(queries.at[lax.rem(r + R - o, R)], a_recv.at[2, o])
    for i in range(2):
        for o in range(R):
            landed(kv.at[i, other, lax.rem(r + R - o, R)], f_recv.at[i, o])

    head = z * R + r
    group = head // Z
    lane0 = pl.multiple_of(lax.rem(head, Z) * hd, hd)
    chunk = Z * STEP
    wide = R * chunk

    def mixed_copy(b, zz):
        return remote(
            mixed.at[b, :, zz],
            mrec.at[b, :, :, pl.ds(lane0, hd)],
            m_send.at[b, zz],
            m_recv.at[lax.rem(head, Z), b],
            device(zz, group, c),
        )

    def attend(b):
        query = queries[:, b * chunk : (b + 1) * chunk, :].reshape(wide, hd)
        best = jnp.full((1, wide), DEAD, f32)
        for cc in range(2):
            for rr in range(R):
                score = lax.dot_general(
                    kv[0, cc, rr], query, (((1,), (1,)), ((), ())), preferred_element_type=f32
                )
                score = score + key_bias[cc, rr]
                scores[cc, rr] = score
                best = jnp.maximum(best, jnp.max(score, axis=0, keepdims=True))
        totals = jnp.zeros((1, wide), f32)
        accum = jnp.zeros((hd, wide), f32)
        for cc in range(2):
            for rr in range(R):
                weight = jnp.exp(scores[cc, rr] - best)
                totals = totals + jnp.sum(weight, axis=0, keepdims=True)
                accum = accum + lax.dot_general(
                    kv[1, cc, rr], weight.astype(bf16), (((0,), (0,)), ((), ())),
                    preferred_element_type=f32,
                )
        mixed[b] = (accum / totals).T.astype(bf16).reshape(R, Z, STEP, hd)
        for zz in range(Z):
            here = jnp.logical_and(z == zz, group == r)

            @pl.when(jnp.logical_not(here))
            def _():
                mixed_copy(b, zz).start()

            @pl.when(here)
            def _():
                mrec[b, :, :, pl.ds(lane0, hd)] = mixed[b, :, zz]

    def project(b):
        for k in range(Z):
            @pl.when(r * Z + k != head)
            def _():
                landed(mrec.at[b, :, :, pl.ds(k * hd, hd)], m_recv.at[k, b])

        for cc in range(2):
            part = jnp.dot(mrec[b].reshape(R * STEP, depth), wo[cc], preferred_element_type=f32)
            parts[b, cc] = part.astype(bf16).reshape(R, STEP, cw)
        dst = got.at[r, c, pl.ds(b * STEP, STEP)]
        for o in range(1, R):
            for oc in range(2):
                j, cc = lax.rem(r + o, R), lax.rem(c + oc, 2)
                push(parts.at[b, cc, j], dst, o_send.at[b, o, oc], o_recv.at[b, o, oc], device(z, j, cc))
        push(parts.at[b, other, r], dst, o_send.at[b, 0, 1], o_recv.at[b, 0, 1], sibling)
        pltpu.make_async_copy(parts.at[b, c, r], dst, o_own.at[b]).start()

    attend(0)
    wo_copy.wait()
    landed(wo.at[other], wo_sem.at[1])
    for b in range(1, blocks):
        attend(b)
        project(b - 1)
    project(blocks - 1)

    for b in range(blocks):
        rows = pl.ds(b * STEP, STEP)
        landed(got.at[r, c, rows], o_own.at[b])
        for o in range(R):
            for oc in range(2):
                if (o, oc) != (0, 0):
                    src = got.at[lax.rem(r + R - o, R), lax.rem(c + oc, 2), rows]
                    landed(src, o_recv.at[b, o, oc])

    for copy in sent:
        copy.wait_send()
    for far in range(Z - 1):
        for up in (True, False):
            @pl.when(passes(up, far))
            def _():
                hop(up, far).wait_send()

    for far in range(1, Z):
        for up in (True, False):
            slab = z - far if up else z + far

            @pl.when(z >= far if up else z + far < Z)
            def _():
                remote(
                    pin.at[slab, pl.ds(pl.multiple_of(other * half, half), half)],
                    pnear.at[slab], near_send.at[slab], near_recv.at[slab], sibling,
                ).wait_send()

    @pl.when(c == owner)
    def _():
        for i in range(3):
            for copy in weight_copies(i):
                copy.wait_send()

    for b in range(blocks):
        for zz in range(Z):
            @pl.when(jnp.logical_not(jnp.logical_and(z == zz, group == r)))
            def _():
                mixed_copy(b, zz).wait_send()


def fused(sizes, patches, visible, ln_gain, ln_bias, w_query, w_key, w_value, w_output):
    Z, R = sizes
    rows, cw = patches.shape
    depth = w_query.shape[0]
    width = depth * R
    half = rows // 2
    hd = HEAD_DIM
    plane = R * hd
    count = Z * half
    blocks = half // STEP
    vmem = pl.BlockSpec(memory_space=pltpu.VMEM)
    hbm = pl.BlockSpec(memory_space=pl.ANY)
    bf, f32, dma = jnp.bfloat16, jnp.float32, pltpu.SemaphoreType.DMA
    got = pl.pallas_call(
        functools.partial(mesh_kernel, (Z, R, hd)),
        out_shape=jax.ShapeDtypeStruct((R, 2, half, cw), bf),
        in_specs=[hbm] + [vmem] * 3 + [hbm] * 4,
        out_specs=hbm,
        scratch_shapes=[
            pltpu.VMEM((Z * R, 8, 128), jnp.int32),
            pltpu.VMEM((count, 1), f32),
            pltpu.VMEM((Z, rows, cw), bf),
            pltpu.VMEM((Z, half, cw), bf),
            pltpu.VMEM((count, width), f32),
            pltpu.VMEM((3, width, plane), bf),
            pltpu.VMEM((2, depth, cw), bf),
            pltpu.VMEM((count, width), bf),
            pltpu.VMEM((3, R, count, hd), bf),
            pltpu.VMEM((R, count, hd), bf),
            pltpu.VMEM((2, 2, R, count, hd), bf),
            pltpu.VMEM((2, R, count, 1), f32),
            pltpu.VMEM((2, R, count, R * Z * STEP), f32),
            pltpu.VMEM((blocks, R, Z, STEP, hd), bf),
            pltpu.VMEM((blocks, R, STEP, depth), bf),
            pltpu.VMEM((blocks, 2, R, STEP, cw), bf),
            dma,
            dma((2, Z)),
            dma((2, Z)),
            dma((Z,)),
            dma((Z,)),
            dma((3,)),
            dma((3, R, 2)),
            dma((3, R)),
            dma((3,)),
            dma((3,)),
            dma((2, 3, R)),
            dma((Z * R,)),
            dma((Z * R,)),
            dma((3, R)),
            dma((3, R)),
            dma((2, R)),
            dma((2, R)),
            dma((blocks, Z)),
            dma((Z, blocks)),
            dma((blocks, R, 2)),
            dma((blocks, R, 2)),
            dma((blocks,)),
        ],
        compiler_params=pltpu.CompilerParams(
            collective_id=0, has_side_effects=True, vmem_limit_bytes=56 * 1024 * 1024
        ),
    )(patches, visible.reshape(1, rows), ln_gain.reshape(1, width), ln_bias.reshape(1, width),
      w_query, w_key, w_value, w_output)
    return jnp.sum(got.astype(f32), axis=0).reshape(rows, cw)


def fits(mesh, patches, w_query):
    Z, R, C = mesh.shape["ctx"], mesh.shape["row"], mesh.shape["col"]
    width = w_query.shape[0]
    half = patches.shape[0] // (Z * R * 2)
    return (
        C == 2
        and Z * R * HEAD_DIM == width
        and (width // C) % (R * HEAD_DIM) == 0
        and width // R == Z * HEAD_DIM
        and half % STEP == 0
        and half <= 128
    )


def solution(mesh):
    placed = (
        P(("ctx", "row"), "col"),
        P(("ctx", "row")),
        P(),
        P(),
        P("row", "col"),
        P("row", "col"),
        P("row", "col"),
        P("row", "col"),
    )

    def run(*args):
        part = body
        if fits(mesh, args[0], args[4]):
            part = functools.partial(fused, (mesh.shape["ctx"], mesh.shape["row"]))
        return jax.shard_map(
            part, mesh=mesh, in_specs=placed, out_specs=P(("ctx", "row"), "col"), check_vma=False
        )(*args)

    return run
```

time: 102 us -> 90.8 us (0.89)
  Pallas kernels: 96.9 us -> 87.8 us
  local copies, waits for them, and re-layouts: 4.21 us -> 0 us
  other arithmetic: 0.72 us -> 2.65 us
    pallas_call x1, Pallas kernels: 96.9 us -> 87.8 us  [fused(): pl.pallas_call(functools.partial(mesh_kernel, (Z, R, hd)), out_shape=jax....]
    unnamed x3 -> x0, local copies, waits for them, and re-layouts: 2.77 us -> none
    reduce_sum x0 -> x1, other arithmetic: none -> 2.65 us  [fused(): return jnp.sum(got.astype(f32), axis=0).reshape(rows, cw)]
where the time goes in v2:
time: 90.8 us; the launch traced here: 90.5 us
  Pallas kernels  87.8 us (97%)
  other arithmetic  2.65 us (3%)
    pallas_call x1, Pallas kernels, fused(): pl.pallas_call(functools.partial(mesh_kernel, (Z, R, hd)), out_shape=jax....  87.8 us
    reduce_sum x1, other arithmetic, fused(): return jnp.sum(got.astype(f32), axis=0).reshape(rows, cw)  2.65 us

profile of v2, /device:TPU:1, one launch (start us, length us, event | category | flops | bytes accessed | tf_op | source)
XLA Modules:
  0.0 90.5 jit_solution(14630236232428809979)
XLA Ops:
  0.0 87.8 %shard_map.82 = bf16[4,2,96,1024]{3,2,1,0:T(8,128)(2,1)} custom-call(bf16[192,1024]{1,0:T(8,128)(2,1)} %patches.1, s32[1,192]{1,0:T(1,128)} %bitcast.6, f32[1,2048]{1,0:T(1,128)} %bitcast.4, f32[1,2048]{1,0:T(1,128)} %bitcast.5, bf16[512,1024]{1,0:T(8,128)(2,1)} %w_query.1, bf16[512,1024]{1,0:T(8,128)(2,1)} %w_key.1, bf16[512,1024]{1,0:T(8,128)(2,1)} %w_value.1, ...), custom_call_target="tpu_custom_call" | custom-call | tf_op jit(solution)/shard_map/pallas_call | solution.py:516
  87.8 2.7 %convert_reduce_fusion = f32[2,96,1024]{2,1,0:T(8,128)} fusion(bf16[4,2,96,1024]{3,2,1,0:T(8,128)(2,1)} %shard_map.82), kind=kLoop, calls=%fused_computation | loop fusion | flops 1376256 | bytes 2359296 | tf_op jit(solution)/shard_map/reduce_sum | solution.py:566

commit v3 on v2

--- a/solution.py
+++ b/solution.py
@@ -13,6 +13,7 @@
 MESH = pl.DeviceIdType.MESH
 DEAD = -1e30
 STEP = 32
+NEAR = (1, 2)
 
 
 def embed(visible, full_width):
@@ -105,10 +106,25 @@
     )
 
 
+def sine(x):
+    turns = jnp.floor(x * (1.0 / math.pi) + 0.5)
+    y = x - turns * 3.140625
+    y = y - turns * 9.67502593994140625e-4
+    y = y - turns * 1.509957990978376432e-7
+    odd = turns - 2.0 * jnp.floor(turns * 0.5)
+    y = y * (1.0 - 2.0 * odd)
+    y2 = y * y
+    tail = y2 * (-1.0 / 39916800.0) + 1.0 / 362880.0
+    tail = tail * y2 - 1.0 / 5040.0
+    tail = tail * y2 + 1.0 / 120.0
+    tail = tail * y2 - 1.0 / 6.0
+    return y + y * y2 * tail
+
+
 def mesh_kernel(
     sizes, patches, vis, gain, bias, w_query, w_key, w_value, w_output, got,
     ids, id_col, pin, pnear, hid, wfull, wo, xs, send, queries, kv, key_bias, scores, mixed, mrec, parts,
-    p_own, z_send, z_recv, near_send, near_recv, wo_sem, w_send, w_recv, w_near, w_own, wf_sem,
+    p_own, z_send, z_recv, near_send, near_recv, wo_sem, w_send, w_recv, w_near, w_own, wf_sem, d_send, d_recv,
     l_send, l_recv, a_send, a_recv, f_send, f_recv, m_send, m_recv, o_send, o_recv, o_own,
 ):
     Z, R, hd = sizes
@@ -192,7 +208,7 @@
         def _():
             hop(up, 0).start()
 
-    weights = (w_key, w_value, w_query)
+    weights = (w_query, w_key, w_value)
     owner = (z * plane) // cw
     col0 = pl.multiple_of(lax.rem(z * plane, cw), plane)
     sub = depth // 2
@@ -200,7 +216,7 @@
     def weight_copies(i):
         src = weights[i]
         copies = []
-        for o in range(1, R):
+        for o in NEAR:
             for cc in range(2):
                 copies.append(
                     remote(
@@ -208,7 +224,7 @@
                         wfull.at[i, pl.ds(pl.multiple_of(r * depth + cc * sub, sub), sub)],
                         w_send.at[i, o, cc],
                         w_recv.at[i, o],
-                        device(z, lax.rem(r + o, R), cc),
+                        device(z, r ^ o, cc),
                     )
                 )
         own = wfull.at[i, pl.ds(pl.multiple_of(r * depth, depth), depth)]
@@ -258,7 +274,7 @@
             coord_y = ((patch_id >> 6) & (GRID - 1)).astype(f32)
             coord_z = (patch_id & (GRID - 1)).astype(f32)
             coord = jnp.where(pick == 0, coord_x, jnp.where(pick == 1, coord_y, coord_z))
-            hid[pl.ds(at, 8), :] = jnp.sin(coord * frequency + phase)
+            hid[pl.ds(at, 8), :] = sine(coord * frequency + phase)
             return carry
 
         lax.fori_loop(0, half // 8, run, 0)
@@ -285,8 +301,33 @@
 
         lax.fori_loop(0, half // 16, run, 0)
 
-    embed_rows(0)
-    embed_rows(half)
+    def weight_rows(i, src_row, cc, part=None):
+        start = src_row * depth + cc * sub
+        if part is None:
+            return wfull.at[i, pl.ds(pl.multiple_of(start, sub), sub)]
+        start = pl.multiple_of(start + part * (sub // 2), sub // 2)
+        return wfull.at[i, pl.ds(start, sub // 2)]
+
+    def weights_on(i):
+        for o in NEAR:
+            landed(weight_rows(i, r ^ o, c), w_recv.at[i, o])
+            step = NEAR[1 - NEAR.index(o)]
+            half_block = weight_rows(i, r ^ o, c, NEAR.index(o))
+            push(half_block, half_block, d_send.at[i, o - 1], d_recv.at[i, o - 1], device(z, r ^ step, c))
+            block = weight_rows(i, r ^ o, c)
+            push(block, block, wf_sem.at[0, i, o], wf_sem.at[1, i, o], sibling)
+
+    def weights_far(i):
+        far = r ^ NEAR[0] ^ NEAR[1]
+        for o in NEAR:
+            landed(weight_rows(i, far, c, NEAR.index(o)), d_recv.at[i, o - 1])
+        block = weight_rows(i, far, c)
+        push(block, block, wf_sem.at[0, i, 3], wf_sem.at[1, i, 3], sibling)
+
+    for zz in range(Z):
+        embed_rows(zz * half)
+    norm_slab(z)
+    weights_on(0)
     for far in range(1, Z):
         for up in (True, False):
             slab = z - far if up else z + far
@@ -308,8 +349,6 @@
                 ).start()
 
         if far == 1:
-            for zz in range(2, Z):
-                embed_rows(zz * half)
             columns = ids[...].astype(f32).reshape(Z * R * 8, 128).T
             dead = jnp.where(columns < 0.0, DEAD, 0.0)
             for zz in range(Z):
@@ -317,7 +356,10 @@
                     for cc in range(2):
                         at = (zz * R + rr) * 8 + cc
                         key_bias[cc, rr, zz * half : (zz + 1) * half, :] = dead[:half, at : at + 1]
-            norm_slab(z)
+        if far <= 2:
+            weights_on(far)
+        if far > 1:
+            weights_far(far - 2)
         for up in (True, False):
             slab = z - far if up else z + far
 
@@ -325,12 +367,7 @@
             def _():
                 norm_slab(slab)
 
-    for i in range(3):
-        for o in range(1, R):
-            src_row = lax.rem(r + R - o, R)
-            block = wfull.at[i, pl.ds(pl.multiple_of(src_row * depth + c * sub, sub), sub)]
-            landed(block, w_recv.at[i, o])
-            push(block, block, wf_sem.at[0, i, o], wf_sem.at[1, i, o], sibling)
+    weights_far(2)
 
     scale = 1.0 / math.sqrt(hd)
     for i in range(3):
@@ -345,17 +382,15 @@
             landed(mine, w_near.at[i])
 
         for o in range(1, R):
-            src_row = lax.rem(r + R - o, R)
-            block = wfull.at[i, pl.ds(pl.multiple_of(src_row * depth + other * sub, sub), sub)]
-            landed(block, wf_sem.at[1, i, o])
+            landed(weight_rows(i, r ^ o, other), wf_sem.at[1, i, o])
         for j in range(0, R, 2):
             pair = jnp.dot(
                 xs[...], wfull[i, :, j * hd : (j + 2) * hd], preferred_element_type=f32
             )
-            if i == 2:
+            if i == 0:
                 pair = pair * scale
             pair = pair.astype(bf16)
-            if i == 2:
+            if i == 0:
                 pair = jnp.concatenate(
                     [
                         pair[zz * half + b * STEP : zz * half + (b + 1) * STEP]
@@ -368,23 +403,20 @@
             send[i, j + 1] = pair[:, hd:]
         for o in range(1, R):
             j = lax.rem(r + o, R)
-            dst = queries.at[r] if i == 2 else kv.at[i, c, r]
+            dst = queries.at[r] if i == 0 else kv.at[i - 1, c, r]
             push(send.at[i, j], dst, a_send.at[i, o], a_recv.at[i, o], device(z, j, c))
-        if i == 2:
+        if i == 0:
             queries[r] = send[i, r]
         else:
-            kv[i, c, r] = send[i, r]
-            push(send.at[i, r], kv.at[i, c, r], f_send.at[i, 0], f_recv.at[i, 0], sibling)
-    for i in range(2):
-        for o in range(1, R):
-            block = kv.at[i, c, lax.rem(r + R - o, R)]
-            landed(block, a_recv.at[i, o])
-            push(block, block, f_send.at[i, o], f_recv.at[i, o], sibling)
+            kv[i - 1, c, r] = send[i, r]
+            push(send.at[i, r], kv.at[i - 1, c, r], f_send.at[i - 1, 0], f_recv.at[i - 1, 0], sibling)
     for o in range(1, R):
-        landed(queries.at[lax.rem(r + R - o, R)], a_recv.at[2, o])
-    for i in range(2):
-        for o in range(R):
-            landed(kv.at[i, other, lax.rem(r + R - o, R)], f_recv.at[i, o])
+        landed(queries.at[lax.rem(r + R - o, R)], a_recv.at[0, o])
+
+    def keys_on(i, o):
+        block = kv.at[i, c, lax.rem(r + R - o, R)]
+        landed(block, a_recv.at[i + 1, o])
+        push(block, block, f_send.at[i, o], f_recv.at[i, o], sibling)
 
     head = z * R + r
     group = head // Z
@@ -404,19 +436,30 @@
     def attend(b):
         query = queries[:, b * chunk : (b + 1) * chunk, :].reshape(wide, hd)
         best = jnp.full((1, wide), DEAD, f32)
-        for cc in range(2):
-            for rr in range(R):
+        for oc in range(2):
+            for o in range(R):
+                cc, rr = lax.rem(c + oc, 2), lax.rem(r + R - o, R)
+                if b == 0 and oc == 0 and o > 0:
+                    keys_on(0, o)
+                if b == 0 and oc == 1:
+                    landed(kv.at[0, cc, rr], f_recv.at[0, o])
                 score = lax.dot_general(
                     kv[0, cc, rr], query, (((1,), (1,)), ((), ())), preferred_element_type=f32
                 )
                 score = score + key_bias[cc, rr]
-                scores[cc, rr] = score
+                scores[oc, o] = score
                 best = jnp.maximum(best, jnp.max(score, axis=0, keepdims=True))
         totals = jnp.zeros((1, wide), f32)
         accum = jnp.zeros((hd, wide), f32)
-        for cc in range(2):
-            for rr in range(R):
-                weight = jnp.exp(scores[cc, rr] - best)
+        if b == 0:
+            for o in range(1, R):
+                keys_on(1, o)
+        for oc in range(2):
+            for o in range(R):
+                cc, rr = lax.rem(c + oc, 2), lax.rem(r + R - o, R)
+                if b == 0 and oc == 1:
+                    landed(kv.at[1, cc, rr], f_recv.at[1, o])
+                weight = jnp.exp(scores[oc, o] - best)
                 totals = totals + jnp.sum(weight, axis=0, keepdims=True)
                 accum = accum + lax.dot_general(
                     kv[1, cc, rr], weight.astype(bf16), (((0,), (0,)), ((), ())),
@@ -546,6 +589,8 @@
             dma((3,)),
             dma((3,)),
             dma((2, 3, R)),
+            dma((3, 2)),
+            dma((3, 2)),
             dma((Z * R,)),
             dma((Z * R,)),
             dma((3, R)),
@@ -572,6 +617,8 @@
     half = patches.shape[0] // (Z * R * 2)
     return (
         C == 2
+        and R == 4
+        and Z == 4
         and Z * R * HEAD_DIM == width
         and (width // C) % (R * HEAD_DIM) == 0
         and width // R == Z * HEAD_DIM

time: 90.8 us -> 86.8 us (0.956)
  Pallas kernels: 87.8 us -> 83.9 us
    pallas_call x1, Pallas kernels: 87.8 us -> 83.9 us  [fused(): pl.pallas_call(functools.partial(mesh_kernel, (Z, R, hd)), out_shape=jax....]
where the time goes in v3:
time: 86.8 us; the launch traced here: 86.6 us
  Pallas kernels  83.9 us (97%)
  other arithmetic  2.65 us (3%)
    pallas_call x1, Pallas kernels, fused(): pl.pallas_call(functools.partial(mesh_kernel, (Z, R, hd)), out_shape=jax....  83.9 us
    reduce_sum x1, other arithmetic, fused(): return jnp.sum(got.astype(f32), axis=0).reshape(rows, cw)  2.65 us

profile of v3, /device:TPU:1, one launch (start us, length us, event | category | flops | bytes accessed | tf_op | source)
XLA Modules:
  0.0 86.6 jit_solution(4139837894444277915)
XLA Ops:
  0.0 83.9 %shard_map.82 = bf16[4,2,96,1024]{3,2,1,0:T(8,128)(2,1)} custom-call(bf16[192,1024]{1,0:T(8,128)(2,1)} %patches.1, s32[1,192]{1,0:T(1,128)} %bitcast.6, f32[1,2048]{1,0:T(1,128)} %bitcast.4, f32[1,2048]{1,0:T(1,128)} %bitcast.5, bf16[512,1024]{1,0:T(8,128)(2,1)} %w_query.1, bf16[512,1024]{1,0:T(8,128)(2,1)} %w_key.1, bf16[512,1024]{1,0:T(8,128)(2,1)} %w_value.1, ...), custom_call_target="tpu_custom_call" | custom-call | tf_op jit(solution)/shard_map/pallas_call | solution.py:559
  83.9 2.7 %convert_reduce_fusion = f32[2,96,1024]{2,1,0:T(8,128)} fusion(bf16[4,2,96,1024]{3,2,1,0:T(8,128)(2,1)} %shard_map.82), kind=kLoop, calls=%fused_computation | loop fusion | flops 1376256 | bytes 2359296 | tf_op jit(solution)/shard_map/reduce_sum | solution.py:611

commit v4 on v3

--- a/solution.py
+++ b/solution.py
@@ -13,6 +13,7 @@
 MESH = pl.DeviceIdType.MESH
 DEAD = -1e30
 STEP = 32
+ONES = 16
 NEAR = (1, 2)
 
 
@@ -123,7 +124,7 @@
 
 def mesh_kernel(
     sizes, patches, vis, gain, bias, w_query, w_key, w_value, w_output, got,
-    ids, id_col, pin, pnear, hid, wfull, wo, xs, send, queries, kv, key_bias, scores, mixed, mrec, parts,
+    ids, id_col, pin, pnear, hid, wfull, wo, xs, send, queries, kv, key_bias, values, scores, mixed, mrec, parts,
     p_own, z_send, z_recv, near_send, near_recv, wo_sem, w_send, w_recv, w_near, w_own, wf_sem, d_send, d_recv,
     l_send, l_recv, a_send, a_recv, f_send, f_recv, m_send, m_recv, o_send, o_recv, o_own,
 ):
@@ -213,35 +214,20 @@
     col0 = pl.multiple_of(lax.rem(z * plane, cw), plane)
     sub = depth // 2
 
-    def weight_copies(i):
-        src = weights[i]
-        copies = []
-        for o in NEAR:
-            for cc in range(2):
-                copies.append(
-                    remote(
-                        src.at[pl.ds(cc * sub, sub), pl.ds(col0, plane)],
-                        wfull.at[i, pl.ds(pl.multiple_of(r * depth + cc * sub, sub), sub)],
-                        w_send.at[i, o, cc],
-                        w_recv.at[i, o],
-                        device(z, r ^ o, cc),
-                    )
-                )
-        own = wfull.at[i, pl.ds(pl.multiple_of(r * depth, depth), depth)]
-        copies.append(
-            remote(src.at[:, pl.ds(col0, plane)], own, w_send.at[i, 0, 0], w_near.at[i], sibling)
-        )
-        return copies
+    own_rows = pl.ds(pl.multiple_of(r * depth, depth), depth)
+
+    def weight_near(i):
+        src = weights[i].at[:, pl.ds(col0, plane)]
+        return remote(src, wfull.at[i, own_rows], w_send.at[i, 0], w_near.at[i], sibling)
 
     def weight_local(i):
-        own = wfull.at[i, pl.ds(pl.multiple_of(r * depth, depth), depth)]
-        return pltpu.make_async_copy(weights[i].at[:, pl.ds(col0, plane)], own, w_own.at[i])
+        src = weights[i].at[:, pl.ds(col0, plane)]
+        return pltpu.make_async_copy(src, wfull.at[i, own_rows], w_own.at[i])
 
     @pl.when(c == owner)
     def _():
         for i in range(3):
-            for copy in weight_copies(i):
-                copy.start()
+            weight_near(i).start()
             weight_local(i).start()
 
     push(w_output, wo.at[c], wo_sem.at[0], wo_sem.at[1], sibling)
@@ -254,6 +240,26 @@
         )
 
     share(z)
+
+    def weight_rows(i, src_row, cc, part=None):
+        start = src_row * depth + cc * sub
+        if part is None:
+            return wfull.at[i, pl.ds(pl.multiple_of(start, sub), sub)]
+        start = pl.multiple_of(start + part * (sub // 2), sub // 2)
+        return wfull.at[i, pl.ds(start, sub // 2)]
+
+    for i in range(3):
+        @pl.when(c == owner)
+        def _():
+            landed(wfull.at[i, own_rows], w_own.at[i])
+
+        @pl.when(c != owner)
+        def _():
+            landed(wfull.at[i, own_rows], w_near.at[i])
+
+        for o in NEAR:
+            block = weight_rows(i, r, c)
+            push(block, block, w_send.at[i, o], w_recv.at[i, o], device(z, r ^ o, c))
 
     for oz in range(Z):
         for orow in range(R):
@@ -301,13 +307,6 @@
 
         lax.fori_loop(0, half // 16, run, 0)
 
-    def weight_rows(i, src_row, cc, part=None):
-        start = src_row * depth + cc * sub
-        if part is None:
-            return wfull.at[i, pl.ds(pl.multiple_of(start, sub), sub)]
-        start = pl.multiple_of(start + part * (sub // 2), sub // 2)
-        return wfull.at[i, pl.ds(start, sub // 2)]
-
     def weights_on(i):
         for o in NEAR:
             landed(weight_rows(i, r ^ o, c), w_recv.at[i, o])
@@ -351,11 +350,14 @@
         if far == 1:
             columns = ids[...].astype(f32).reshape(Z * R * 8, 128).T
             dead = jnp.where(columns < 0.0, DEAD, 0.0)
+            first = lax.broadcasted_iota(jnp.int32, (half, hd), 1) == 0
             for zz in range(Z):
                 for rr in range(R):
                     for cc in range(2):
                         at = (zz * R + rr) * 8 + cc
-                        key_bias[cc, rr, zz * half : (zz + 1) * half, :] = dead[:half, at : at + 1]
+                        key_bias[cc, rr, zz * half : (zz + 1) * half, :] = jnp.where(
+                            first, dead[:half, at : at + 1], 0.0
+                        ).astype(bf16)
         if far <= 2:
             weights_on(far)
         if far > 1:
@@ -369,18 +371,8 @@
 
     weights_far(2)
 
-    scale = 1.0 / math.sqrt(hd)
+    scale = math.log2(math.e) / math.sqrt(hd)
     for i in range(3):
-        mine = wfull.at[i, pl.ds(pl.multiple_of(r * depth, depth), depth)]
-
-        @pl.when(c == owner)
-        def _():
-            landed(mine, w_own.at[i])
-
-        @pl.when(c != owner)
-        def _():
-            landed(mine, w_near.at[i])
-
         for o in range(1, R):
             landed(weight_rows(i, r ^ o, other), wf_sem.at[1, i, o])
         for j in range(0, R, 2):
@@ -433,8 +425,11 @@
             device(zz, group, c),
         )
 
+    lane = lax.broadcasted_iota(jnp.int32, (wide, hd), 1)
+
     def attend(b):
         query = queries[:, b * chunk : (b + 1) * chunk, :].reshape(wide, hd)
+        query = jnp.concatenate([query, (lane == 0).astype(bf16)], axis=1)
         best = jnp.full((1, wide), DEAD, f32)
         for oc in range(2):
             for o in range(R):
@@ -443,14 +438,13 @@
                     keys_on(0, o)
                 if b == 0 and oc == 1:
                     landed(kv.at[0, cc, rr], f_recv.at[0, o])
+                keys = jnp.concatenate([kv[0, cc, rr], key_bias[cc, rr]], axis=1)
                 score = lax.dot_general(
-                    kv[0, cc, rr], query, (((1,), (1,)), ((), ())), preferred_element_type=f32
+                    keys, query, (((1,), (1,)), ((), ())), preferred_element_type=f32
                 )
-                score = score + key_bias[cc, rr]
                 scores[oc, o] = score
                 best = jnp.maximum(best, jnp.max(score, axis=0, keepdims=True))
-        totals = jnp.zeros((1, wide), f32)
-        accum = jnp.zeros((hd, wide), f32)
+        accum = jnp.zeros((hd + ONES, wide), f32)
         if b == 0:
             for o in range(1, R):
                 keys_on(1, o)
@@ -459,13 +453,12 @@
                 cc, rr = lax.rem(c + oc, 2), lax.rem(r + R - o, R)
                 if b == 0 and oc == 1:
                     landed(kv.at[1, cc, rr], f_recv.at[1, o])
-                weight = jnp.exp(scores[oc, o] - best)
-                totals = totals + jnp.sum(weight, axis=0, keepdims=True)
-                accum = accum + lax.dot_general(
-                    kv[1, cc, rr], weight.astype(bf16), (((0,), (0,)), ((), ())),
-                    preferred_element_type=f32,
-                )
-        mixed[b] = (accum / totals).T.astype(bf16).reshape(R, Z, STEP, hd)
+                if b == 0:
+                    values[oc, o, :hd] = kv[1, cc, rr].T
+                    values[oc, o, hd:] = jnp.ones((ONES, count), bf16)
+                weight = jnp.exp2(scores[oc, o] - best).astype(bf16)
+                accum = accum + jnp.dot(values[oc, o], weight, preferred_element_type=f32)
+        mixed[b] = (accum[:hd] / accum[hd : hd + 1]).T.astype(bf16).reshape(R, Z, STEP, hd)
         for zz in range(Z):
             here = jnp.logical_and(z == zz, group == r)
 
@@ -533,8 +526,7 @@
     @pl.when(c == owner)
     def _():
         for i in range(3):
-            for copy in weight_copies(i):
-                copy.wait_send()
+            weight_near(i).wait_send()
 
     for b in range(blocks):
         for zz in range(Z):
@@ -573,7 +565,8 @@
             pltpu.VMEM((3, R, count, hd), bf),
             pltpu.VMEM((R, count, hd), bf),
             pltpu.VMEM((2, 2, R, count, hd), bf),
-            pltpu.VMEM((2, R, count, 1), f32),
+            pltpu.VMEM((2, R, count, hd), bf),
+            pltpu.VMEM((2, R, hd + ONES, count), bf),
             pltpu.VMEM((2, R, count, R * Z * STEP), f32),
             pltpu.VMEM((blocks, R, Z, STEP, hd), bf),
             pltpu.VMEM((blocks, R, STEP, depth), bf),
@@ -584,7 +577,7 @@
             dma((Z,)),
             dma((Z,)),
             dma((3,)),
-            dma((3, R, 2)),
+            dma((3, R)),
             dma((3, R)),
             dma((3,)),
             dma((3,)),

time: 86.8 us -> 89.6 us (1.032)
  Pallas kernels: 83.9 us -> 86.7 us
    pallas_call x1, Pallas kernels: 83.9 us -> 86.7 us  [fused(): pl.pallas_call(functools.partial(mesh_kernel, (Z, R, hd)), out_shape=jax....]
where the time goes in v4:
time: 89.6 us; the launch traced here: 89.4 us
  Pallas kernels  86.7 us (97%)
  other arithmetic  2.65 us (3%)
    pallas_call x1, Pallas kernels, fused(): pl.pallas_call(functools.partial(mesh_kernel, (Z, R, hd)), out_shape=jax....  86.7 us
    reduce_sum x1, other arithmetic, fused(): return jnp.sum(got.astype(f32), axis=0).reshape(rows, cw)  2.65 us

profile of v4, /device:TPU:1, one launch (start us, length us, event | category | flops | bytes accessed | tf_op | source)
XLA Modules:
  0.0 89.4 jit_solution(14642828688094780445)
XLA Ops:
  0.0 86.7 %shard_map.82 = bf16[4,2,96,1024]{3,2,1,0:T(8,128)(2,1)} custom-call(bf16[192,1024]{1,0:T(8,128)(2,1)} %patches.1, s32[1,192]{1,0:T(1,128)} %bitcast.6, f32[1,2048]{1,0:T(1,128)} %bitcast.4, f32[1,2048]{1,0:T(1,128)} %bitcast.5, bf16[512,1024]{1,0:T(8,128)(2,1)} %w_query.1, bf16[512,1024]{1,0:T(8,128)(2,1)} %w_key.1, bf16[512,1024]{1,0:T(8,128)(2,1)} %w_value.1, ...), custom_call_target="tpu_custom_call" | custom-call | tf_op jit(solution)/shard_map/pallas_call | solution.py:551
  86.7 2.7 %convert_reduce_fusion = f32[2,96,1024]{2,1,0:T(8,128)} fusion(bf16[4,2,96,1024]{3,2,1,0:T(8,128)(2,1)} %shard_map.82), kind=kLoop, calls=%fused_computation | loop fusion | flops 1376256 | bytes 2359296 | tf_op jit(solution)/shard_map/reduce_sum | solution.py:604

commit v5 on v4

--- a/solution.py
+++ b/solution.py
@@ -216,18 +216,35 @@
 
     own_rows = pl.ds(pl.multiple_of(r * depth, depth), depth)
 
-    def weight_near(i):
-        src = weights[i].at[:, pl.ds(col0, plane)]
-        return remote(src, wfull.at[i, own_rows], w_send.at[i, 0], w_near.at[i], sibling)
+    def weight_copies(i):
+        src = weights[i]
+        copies = []
+        for o in NEAR:
+            for cc in range(2):
+                copies.append(
+                    remote(
+                        src.at[pl.ds(cc * sub, sub), pl.ds(col0, plane)],
+                        wfull.at[i, pl.ds(pl.multiple_of(r * depth + cc * sub, sub), sub)],
+                        w_send.at[i, o, cc],
+                        w_recv.at[i, o],
+                        device(z, r ^ o, cc),
+                    )
+                )
+        own = wfull.at[i, pl.ds(pl.multiple_of(r * depth, depth), depth)]
+        copies.append(
+            remote(src.at[:, pl.ds(col0, plane)], own, w_send.at[i, 0, 0], w_near.at[i], sibling)
+        )
+        return copies
 
     def weight_local(i):
-        src = weights[i].at[:, pl.ds(col0, plane)]
-        return pltpu.make_async_copy(src, wfull.at[i, own_rows], w_own.at[i])
+        own = wfull.at[i, pl.ds(pl.multiple_of(r * depth, depth), depth)]
+        return pltpu.make_async_copy(weights[i].at[:, pl.ds(col0, plane)], own, w_own.at[i])
 
     @pl.when(c == owner)
     def _():
         for i in range(3):
-            weight_near(i).start()
+            for copy in weight_copies(i):
+                copy.start()
             weight_local(i).start()
 
     push(w_output, wo.at[c], wo_sem.at[0], wo_sem.at[1], sibling)
@@ -247,19 +264,6 @@
             return wfull.at[i, pl.ds(pl.multiple_of(start, sub), sub)]
         start = pl.multiple_of(start + part * (sub // 2), sub // 2)
         return wfull.at[i, pl.ds(start, sub // 2)]
-
-    for i in range(3):
-        @pl.when(c == owner)
-        def _():
-            landed(wfull.at[i, own_rows], w_own.at[i])
-
-        @pl.when(c != owner)
-        def _():
-            landed(wfull.at[i, own_rows], w_near.at[i])
-
-        for o in NEAR:
-            block = weight_rows(i, r, c)
-            push(block, block, w_send.at[i, o], w_recv.at[i, o], device(z, r ^ o, c))
 
     for oz in range(Z):
         for orow in range(R):
@@ -326,7 +330,6 @@
     for zz in range(Z):
         embed_rows(zz * half)
     norm_slab(z)
-    weights_on(0)
     for far in range(1, Z):
         for up in (True, False):
             slab = z - far if up else z + far
@@ -358,10 +361,11 @@
                         key_bias[cc, rr, zz * half : (zz + 1) * half, :] = jnp.where(
                             first, dead[:half, at : at + 1], 0.0
                         ).astype(bf16)
-        if far <= 2:
-            weights_on(far)
-        if far > 1:
-            weights_far(far - 2)
+        if far == 2:
+            for i in range(3):
+                weights_on(i)
+            for i in range(2):
+                weights_far(i)
         for up in (True, False):
             slab = z - far if up else z + far
 
@@ -373,6 +377,14 @@
 
     scale = math.log2(math.e) / math.sqrt(hd)
     for i in range(3):
+        @pl.when(c == owner)
+        def _():
+            landed(wfull.at[i, own_rows], w_own.at[i])
+
+        @pl.when(c != owner)
+        def _():
+            landed(wfull.at[i, own_rows], w_near.at[i])
+
         for o in range(1, R):
             landed(weight_rows(i, r ^ o, other), wf_sem.at[1, i, o])
         for j in range(0, R, 2):
@@ -526,7 +538,8 @@
     @pl.when(c == owner)
     def _():
         for i in range(3):
-            weight_near(i).wait_send()
+            for copy in weight_copies(i):
+                copy.wait_send()
 
     for b in range(blocks):
         for zz in range(Z):
@@ -577,7 +590,7 @@
             dma((Z,)),
             dma((Z,)),
             dma((3,)),
-            dma((3, R)),
+            dma((3, R, 2)),
             dma((3, R)),
             dma((3,)),
             dma((3,)),

time: 89.6 us -> 85.7 us (0.956)
  Pallas kernels: 86.7 us -> 82.7 us
    pallas_call x1, Pallas kernels: 86.7 us -> 82.7 us  [fused(): pl.pallas_call(functools.partial(mesh_kernel, (Z, R, hd)), out_shape=jax....]
where the time goes in v5:
time: 85.7 us; the launch traced here: 85.4 us
  Pallas kernels  82.7 us (96%)
  other arithmetic  2.65 us (3%)
    pallas_call x1, Pallas kernels, fused(): pl.pallas_call(functools.partial(mesh_kernel, (Z, R, hd)), out_shape=jax....  82.7 us
    reduce_sum x1, other arithmetic, fused(): return jnp.sum(got.astype(f32), axis=0).reshape(rows, cw)  2.65 us

profile of v5, /device:TPU:1, one launch (start us, length us, event | category | flops | bytes accessed | tf_op | source)
XLA Modules:
  0.0 85.4 jit_solution(1877379202759922291)
XLA Ops:
  0.0 82.7 %shard_map.82 = bf16[4,2,96,1024]{3,2,1,0:T(8,128)(2,1)} custom-call(bf16[192,1024]{1,0:T(8,128)(2,1)} %patches.1, s32[1,192]{1,0:T(1,128)} %bitcast.6, f32[1,2048]{1,0:T(1,128)} %bitcast.4, f32[1,2048]{1,0:T(1,128)} %bitcast.5, bf16[512,1024]{1,0:T(8,128)(2,1)} %w_query.1, bf16[512,1024]{1,0:T(8,128)(2,1)} %w_key.1, bf16[512,1024]{1,0:T(8,128)(2,1)} %w_value.1, ...), custom_call_target="tpu_custom_call" | custom-call | tf_op jit(solution)/shard_map/pallas_call | solution.py:564
  82.7 2.7 %convert_reduce_fusion = f32[2,96,1024]{2,1,0:T(8,128)} fusion(bf16[4,2,96,1024]{3,2,1,0:T(8,128)(2,1)} %shard_map.82), kind=kLoop, calls=%fused_computation | loop fusion | flops 1376256 | bytes 2359296 | tf_op jit(solution)/shard_map/reduce_sum | solution.py:617

commit v6 on v5

--- a/solution.py
+++ b/solution.py
@@ -12,7 +12,7 @@
 GRID = 64
 MESH = pl.DeviceIdType.MESH
 DEAD = -1e30
-STEP = 32
+STEP = 16
 ONES = 16
 NEAR = (1, 2)
 

time: 85.7 us -> 88.2 us (1.029)
  Pallas kernels: 82.7 us -> 85.1 us
    pallas_call x1, Pallas kernels: 82.7 us -> 85.1 us  [fused(): pl.pallas_call(functools.partial(mesh_kernel, (Z, R, hd)), out_shape=jax....]
where the time goes in v6:
time: 88.2 us; the launch traced here: 87.7 us
  Pallas kernels  85.1 us (96%)
  other arithmetic  2.65 us (3%)
    pallas_call x1, Pallas kernels, fused(): pl.pallas_call(functools.partial(mesh_kernel, (Z, R, hd)), out_shape=jax....  85.1 us
    reduce_sum x1, other arithmetic, fused(): return jnp.sum(got.astype(f32), axis=0).reshape(rows, cw)  2.65 us

profile of v6, /device:TPU:1, one launch (start us, length us, event | category | flops | bytes accessed | tf_op | source)
XLA Modules:
  0.0 87.7 jit_solution(8572551068900408521)
XLA Ops:
  0.0 85.1 %shard_map.82 = bf16[4,2,96,1024]{3,2,1,0:T(8,128)(2,1)} custom-call(bf16[192,1024]{1,0:T(8,128)(2,1)} %patches.1, s32[1,192]{1,0:T(1,128)} %bitcast.6, f32[1,2048]{1,0:T(1,128)} %bitcast.4, f32[1,2048]{1,0:T(1,128)} %bitcast.5, bf16[512,1024]{1,0:T(8,128)(2,1)} %w_query.1, bf16[512,1024]{1,0:T(8,128)(2,1)} %w_key.1, bf16[512,1024]{1,0:T(8,128)(2,1)} %w_value.1, ...), custom_call_target="tpu_custom_call" | custom-call | tf_op jit(solution)/shard_map/pallas_call | solution.py:564
  85.1 2.7 %convert_reduce_fusion = f32[2,96,1024]{2,1,0:T(8,128)} fusion(bf16[4,2,96,1024]{3,2,1,0:T(8,128)(2,1)} %shard_map.82), kind=kLoop, calls=%fused_computation | loop fusion | flops 1376256 | bytes 2359296 | tf_op jit(solution)/shard_map/reduce_sum | solution.py:617

commit v7 on v5

--- a/solution.py
+++ b/solution.py
@@ -456,6 +456,8 @@
                 )
                 scores[oc, o] = score
                 best = jnp.maximum(best, jnp.max(score, axis=0, keepdims=True))
+        if b > 0:
+            project(b - 1)
         accum = jnp.zeros((hd + ONES, wide), f32)
         if b == 0:
             for o in range(1, R):
@@ -504,7 +506,6 @@
     landed(wo.at[other], wo_sem.at[1])
     for b in range(1, blocks):
         attend(b)
-        project(b - 1)
     project(blocks - 1)
 
     for b in range(blocks):

time: 85.7 us -> 88.5 us (1.033)
  Pallas kernels: 82.7 us -> 85.6 us
    pallas_call x1, Pallas kernels: 82.7 us -> 85.6 us  [fused(): pl.pallas_call(functools.partial(mesh_kernel, (Z, R, hd)), out_shape=jax....]
where the time goes in v7:
time: 88.5 us; the launch traced here: 88.3 us
  Pallas kernels  85.6 us (97%)
  other arithmetic  2.65 us (3%)
    pallas_call x1, Pallas kernels, fused(): pl.pallas_call(functools.partial(mesh_kernel, (Z, R, hd)), out_shape=jax....  85.6 us
    reduce_sum x1, other arithmetic, fused(): return jnp.sum(got.astype(f32), axis=0).reshape(rows, cw)  2.65 us

profile of v7, /device:TPU:1, one launch (start us, length us, event | category | flops | bytes accessed | tf_op | source)
XLA Modules:
  0.0 88.3 jit_solution(9568415602919584350)
XLA Ops:
  0.0 85.6 %shard_map.82 = bf16[4,2,96,1024]{3,2,1,0:T(8,128)(2,1)} custom-call(bf16[192,1024]{1,0:T(8,128)(2,1)} %patches.1, s32[1,192]{1,0:T(1,128)} %bitcast.6, f32[1,2048]{1,0:T(1,128)} %bitcast.4, f32[1,2048]{1,0:T(1,128)} %bitcast.5, bf16[512,1024]{1,0:T(8,128)(2,1)} %w_query.1, bf16[512,1024]{1,0:T(8,128)(2,1)} %w_key.1, bf16[512,1024]{1,0:T(8,128)(2,1)} %w_value.1, ...), custom_call_target="tpu_custom_call" | custom-call | tf_op jit(solution)/shard_map/pallas_call | solution.py:565
  85.6 2.7 %convert_reduce_fusion = f32[2,96,1024]{2,1,0:T(8,128)} fusion(bf16[4,2,96,1024]{3,2,1,0:T(8,128)(2,1)} %shard_map.82), kind=kLoop, calls=%fused_computation | loop fusion | flops 1376256 | bytes 2359296 | tf_op jit(solution)/shard_map/reduce_sum | solution.py:618
